TPU v7x, 256 devices: a whole 4x4x8 slice. The times are simulated.
256 devices in a mesh: lat: 32 (over x, z), lon: 8 (over y, core).
Axes of the slice: x: 4, y: 4, z: 8, core: 2. Of those that a mesh axis runs over, the one named last changes fastest.
Arguments:
- prior: float32 [512, 128, 16, 128], P('lat', 'lon'), may hold values from -6 to 6
- stencil_rows: int32 [2, 1024, 4], replicated, may hold values from 0 to 1048560, as said below
- obs_frac: float32 [2, 1024, 2], replicated, may hold values from 0 to 1
- obs_value: float32 [2, 1024], replicated, may hold values from -6 to 6
- obs_var: float32 [2, 1024], replicated, may hold values from 0.25 to 2
Outputs:
- posterior: float32 [512, 128, 16, 128], P('lat', 'lon')
Inputs may be any that keep to these rules, and one draw needn't show every extreme that they name: `stencil_rows`: each observation's four rows are the level-0 corners of one grid cell: (a, b), (a + 1, b), (a, b + 1), (a + 1, b + 1) in latitude and longitude, longitude periodic over 128, a at most 510; row = (latitude * 128 + longitude) * 16.
All inputs are finite; a program needn't handle non-finite values.
Results may differ from a plain program's by a relative error of at most 0.0003.
Values sent between devices are 32-bit elements; how exact they have to be, the bound alone decides.
A program may use at most 128 MiB of HBM per device.

v0:
```python
import jax
import jax.numpy as jnp
from jax import lax
from jax.sharding import PartitionSpec as P


def from_root(x, axis, root):
    mine = lax.axis_index(axis) == root
    return lax.psum(jnp.where(mine, x, jnp.zeros_like(x)), axis)


def taper_gc(distance, radius):
    scaled = distance / radius
    inner_part = (
        ((-0.25 * scaled + 0.5) * scaled + 0.625) * scaled - 5.0 / 3.0
    ) * scaled * scaled + 1.0
    outer_part = (
        ((((scaled / 12.0 - 0.5) * scaled + 0.625) * scaled + 5.0 / 3.0) * scaled - 5.0) * scaled
        + 4.0
        - 2.0 / (3.0 * jnp.maximum(scaled, 1.0))
    )
    return jnp.where(scaled <= 1.0, inner_part, jnp.where(scaled <= 2.0, outer_part, 0.0))


def geometry(stencil, fraction, total_lon, levels):
    corner = stencil[:, 0] // levels
    base_lat = corner // total_lon
    base_lon = corner % total_lon
    frac_lat = fraction[:, 0]
    frac_lon = fraction[:, 1]
    weights = jnp.stack(
        [
            (1.0 - frac_lat) * (1.0 - frac_lon),
            frac_lat * (1.0 - frac_lon),
            (1.0 - frac_lat) * frac_lon,
            frac_lat * frac_lon,
        ],
        axis=-1,
    )
    obs_lat = base_lat.astype(jnp.float32) + frac_lat
    obs_lon = base_lon.astype(jnp.float32) + frac_lon
    return (weights, obs_lat, obs_lon)


def solve_spread(observed, value, variance, members):
    obs_mean = jnp.mean(observed, axis=-1)
    obs_anom = observed - obs_mean[:, None]
    innovation = value - obs_mean
    system = jnp.dot(obs_anom, obs_anom.T, precision=lax.Precision.HIGHEST) / (
        members - 1.0
    ) + jnp.diag(variance)
    factor = jnp.linalg.cholesky(system)
    mean_part = jax.scipy.linalg.cho_solve((factor, True), innovation)
    anom_part = jax.scipy.linalg.cho_solve((factor, True), obs_anom)
    return mean_part[:, None] - 0.5 * anom_part


def local(prior, stencil_rows, obs_frac, obs_value, obs_var):
    lon_count = lax.axis_size("lon")
    lat_cells, lon_cells, levels, members = prior.shape
    total_lon = lon_cells * lon_count
    own_lat = lax.axis_index("lat")
    own_lon = lax.axis_index("lon")
    radius = lat_cells * 1.0
    lat_coord = (own_lat * lat_cells + jnp.arange(lat_cells)).astype(jnp.float32)
    lon_coord = (own_lon * lon_cells + jnp.arange(lon_cells)).astype(jnp.float32)
    ensemble = prior
    for batch_idx in range(stencil_rows.shape[0]):
        stencil = stencil_rows[batch_idx]
        value = obs_value[batch_idx]
        variance = obs_var[batch_idx]
        weights, obs_lat, obs_lon = geometry(stencil, obs_frac[batch_idx], total_lon, levels)
        column = stencil // levels
        grid_lat = column // total_lon
        grid_lon = column % total_lon
        is_owned = (grid_lat // lat_cells == own_lat) & (grid_lon // lon_cells == own_lon)
        local_idx = grid_lat % lat_cells * lon_cells + grid_lon % lon_cells
        surface = ensemble[:, :, 0, :].reshape(lat_cells * lon_cells, members)
        picked = surface[local_idx]
        partial_obs = jnp.sum(jnp.where(is_owned, weights, 0.0)[:, :, None] * picked, axis=1)
        observed = lax.psum(partial_obs, ("lat", "lon"))
        obs_anom = observed - jnp.mean(observed, axis=-1, keepdims=True)
        first_column = stencil[0, 0] // levels
        leader = (
            first_column // total_lon // lat_cells * lon_count
            + first_column % total_lon // lon_cells
        )

        def solve_here():
            return solve_spread(observed, value, variance, members)

        def skip_solve():
            return jnp.zeros(observed.shape, jnp.float32)

        spread = lax.cond(own_lat * lon_count + own_lon == leader, solve_here, skip_solve)
        spread = from_root(spread, ("lat", "lon"), leader)
        lat_diff = lat_coord[:, None] - obs_lat[None, :]
        lon_diff = jnp.abs(lon_coord[:, None] - obs_lon[None, :])
        lon_diff = jnp.minimum(lon_diff, total_lon - lon_diff)
        distance = jnp.sqrt(
            lat_diff[:, None, :] * lat_diff[:, None, :]
            + lon_diff[None, :, :] * lon_diff[None, :, :]
        )
        taper = taper_gc(distance, radius).reshape(lat_cells * lon_cells, -1)
        by_level = jnp.moveaxis(ensemble.reshape(lat_cells * lon_cells, levels, members), 1, 0)

        def update_level(level_state):
            anomaly = level_state - jnp.mean(level_state, axis=-1, keepdims=True)
            covariance = jnp.dot(anomaly, obs_anom.T, precision=lax.Precision.HIGHEST) / (
                members - 1.0
            )
            covariance = covariance * taper
            return level_state + jnp.dot(covariance, spread, precision=lax.Precision.HIGHEST)

        by_level = lax.map(update_level, by_level)
        ensemble = jnp.moveaxis(by_level, 0, 1).reshape(lat_cells, lon_cells, levels, members)
    return ensemble


def solution(mesh):
    placed = (P("lat", "lon", None, None), P(), P(), P(), P())
    return jax.shard_map(
        local, mesh=mesh, in_specs=placed, out_specs=P("lat", "lon", None, None), check_vma=False
    )
```

profile of v0, /device:TPU:1, one launch (start us, length us, event | category | flops | bytes accessed | tf_op | source)
XLA Modules:
  0.0 1986.9 jit_solution(7804611628476076133)
XLA Ops:
  11.2 10.8 gather_fusion
  22.0 6.4 multiply_reduce_fusion.1
  32.3 3.6 copy.18
  37.1 246.0 %all-reduce.6.cloned.1.call-done = f32[1024,128]{1,0:T(8,128)} async-done(((f32[1024,128]{1,0:T(8,128)}), f32[1024,128]{1,0:T(8,128)}) %all-reduce.6.cloned.1.call-update) | async-done | bytes 524304 | tf_op jit(solution)/shard_map/psum | solution.py:81
  283.0 6.7 conditional.2
  292.2 602.3 %all-reduce.8.cloned.1.call-done = f32[1024,128]{1,0:T(8,128)} async-done(((f32[1024,128]{1,0:T(8,128)}), f32[1024,128]{1,0:T(8,128)}) %all-reduce.8.cloned.1.call-update) | async-done | bytes 524304 | tf_op jit(solution)/shard_map/psum | solution.py:9
  894.7 101.2 %while.32 = (s32[]{:T(128)}, f32[16,256,128]{2,1,0:T(8,128)S(1)}, f32[16,256,128]{2,1,0:T(8,128)}, f32[1024,128]{1,0:T(8,128)S(1)}, f32[1024,128]{1,0:T(8,128)},...) while((s32[]{:T(128)}, f32[16,256,128]{2,1,0:T(8,128)S(1)}, ...), condition=%wide.region_25.29_spmd.clone, body=%wide.region_23.28_spmd.clone.sunk | while | flops 813531136 | bytes 17437304 | solution.py:115
  997.2 10.8 gather_fusion.1
  1008.0 6.4 multiply_reduce_fusion
  1017.7 247.7 %all-reduce.10.cloned.1.call-done = f32[1024,128]{1,0:T(8,128)} async-done(((f32[1024,128]{1,0:T(8,128)}), f32[1024,128]{1,0:T(8,128)}) %all-reduce.10.cloned.1.call-update) | async-done | bytes 524304 | tf_op jit(solution)/shard_map/psum | solution.py:81
  1265.4 4.5 conditional.3
  1272.2 604.1 %all-reduce.12.cloned.1.call-done = f32[1024,128]{1,0:T(8,128)} async-done(((f32[1024,128]{1,0:T(8,128)}), f32[1024,128]{1,0:T(8,128)}) %all-reduce.12.cloned.1.call-update) | async-done | bytes 524304 | tf_op jit(solution)/shard_map/psum | solution.py:9
  1876.5 101.2 %while.33 = (s32[]{:T(128)}, f32[16,256,128]{2,1,0:T(8,128)S(1)}, f32[16,256,128]{2,1,0:T(8,128)}, f32[1024,128]{1,0:T(8,128)S(1)}, f32[1024,128]{1,0:T(8,128)},...) while((s32[]{:T(128)}, f32[16,256,128]{2,1,0:T(8,128)S(1)}, ...), condition=%wide.region_35.39_spmd.clone, body=%wide.region_33.38_spmd.clone.sunk | while | flops 813531136 | bytes 17437304 | solution.py:115
  1885.1 2.1 fusion.596
  1891.4 2.1 fusion.596
  1897.8 2.1 fusion.596
  1904.1 2.1 fusion.596
  1910.4 2.1 fusion.596
  1916.7 2.1 fusion.596
  1923.0 2.1 fusion.596
  1929.4 2.1 fusion.596
  1935.7 2.1 fusion.596
  1942.0 2.1 fusion.596
  1977.7 2.5 copy.23
  (305 shorter events, 193.1 us)
Async XLA Ops:
  6.5 276.5 %all-reduce.6.cloned.1.call-start = ((), (), s32[]{:S(2)}) async-start(), calls=%async_computation | async-start | bytes 1048576 | tf_op jit(solution)/shard_map/psum | solution.py:81
  11.2 17.3 copy-start.10
  28.4 254.6 %copy-start.11 = (f32[2,1024]{1,0:T(2,128)S(1)}, f32[2,1024]{1,0:T(2,128)}, u32[]{:S(2)}) copy-start(f32[2,1024]{1,0:T(2,128)} %param.22) | copy-start | bytes 24580
  28.4 254.6 %copy-start.12 = (f32[2,1024]{1,0:T(2,128)S(1)}, f32[2,1024]{1,0:T(2,128)}, u32[]{:S(2)}) copy-start(f32[2,1024]{1,0:T(2,128)} %param.21) | copy-start | bytes 24580
  28.4 866.0 %all-reduce.8.cloned.1.call-start = ((), (), s32[]{:S(2)}) async-start(), calls=%async_computation.1 | async-start | bytes 1048576 | tf_op jit(solution)/shard_map/psum | solution.py:9
  283.0 8.9 copy-start.7
  290.6 974.7 %all-reduce.10.cloned.1.call-start = ((), (), s32[]{:S(2)}) async-start(), calls=%async_computation.2 | async-start | bytes 1048576 | tf_op jit(solution)/shard_map/psum | solution.py:81
  997.2 10.8 copy-start.9
  1014.4 861.9 %all-reduce.12.cloned.1.call-start = ((), (), s32[]{:S(2)}) async-start(), calls=%async_computation.3 | async-start | bytes 1048576 | tf_op jit(solution)/shard_map/psum | solution.py:9
  1265.4 6.6 copy-start.8
  1883.4 3.8 copy-start.2
  1889.7 3.8 copy-start.2
  1896.0 3.8 copy-start.2
  1902.4 3.8 copy-start.2
  1908.7 3.8 copy-start.2
  1915.0 3.8 copy-start.2
  1921.3 3.8 copy-start.2
  1927.7 3.8 copy-start.2
  1934.0 3.8 copy-start.2
  1940.3 3.8 copy-start.2
  1946.6 3.8 copy-start.2
  1953.0 3.8 copy-start.2
  1959.3 3.8 copy-start.2
  1965.6 3.8 copy-start.2
  (19 other events, 70.3 us)
Sparse Core Ops, SparseCore 0:
  28.6 254.4 all-reduce.5
  290.7 603.6 all-reduce.7
  1014.5 250.7 all-reduce.9
  1270.8 605.3 all-reduce.11
where the time goes:
time: 2000 us; the launch traced here: 1990 us
  waiting for transfers between devices  1700 us (85%)
  matrix products  128 us (6%)
  other arithmetic  91.4 us (5%)
  local copies, waits for them, and re-layouts  35 us (2%)
    psum x2, waiting for transfers between devices, from_root(): return lax.psum(jnp.where(mine, x, jnp.zeros_like(x)), axis)  1210 us
    psum x2, waiting for transfers between devices, local(): observed = lax.psum(partial_obs, ('lat', 'lon'))  494 us
    dot_general x32, matrix products, update_level(): jnp.dot(anomaly, obs_anom.T, precision=lax.Precision.HIGHEST)  67.3 us
    dot_general x32, matrix products, update_level(): jnp.dot(covariance, spread, precision=lax.Precision.HIGHEST)  60.8 us
  transfers between devices with their start and end apart: 4, of which 4 were waited for; matrix products, arithmetic and copies ran while one was open for 0% of the time, Pallas kernels for 0%

commit v1 on v0

v1 whole, which is shorter than its diff:
```python
import functools

import jax
import jax.numpy as jnp
from jax import lax
from jax.experimental import pallas as pl
from jax.experimental.pallas import tpu as pltpu
from jax.sharding import PartitionSpec as P

MESH = pl.DeviceIdType.MESH
F32, BF16 = jnp.float32, jnp.bfloat16
HIGHEST = lax.Precision.HIGHEST
NX, NY, NZ, NC = 4, 4, 8, 2
CL = 16
DEPTH = 16
MEM = 128
NOBS = 1024
NLON = 128
BLK = 128
NB = NOBS // BLK
HB = NB // NC
ROWS = 8
TL = 4


def split(v):
    hi = v.astype(BF16)
    return hi, (v - hi.astype(F32)).astype(BF16)


def split3(v):
    hi = v.astype(BF16)
    rest = v - hi.astype(F32)
    mid = rest.astype(BF16)
    return hi, mid, (rest - mid.astype(F32)).astype(BF16)


def mm(a, b):
    return jnp.dot(a, b, preferred_element_type=F32)


def mm_nt(a, b, precision=None):
    return lax.dot_general(
        a, b, (((1,), (1,)), ((), ())), preferred_element_type=F32, precision=precision
    )


def place():
    lat, lon = lax.axis_index("lat"), lax.axis_index("lon")
    return lat // NZ, lon // NC, lat % NZ, lon % NC


def device(x, y, z, c):
    return (x * NZ + z, y * NC + c)


def observe_kernel(
    bi, ens, st, fr, out, surf, part, got1, acc, got2, local_sem, send, recv
):
    x, y, z, c = place()
    q = x * NY + y
    plane = []
    for r in range(1, NX * NY):
        px, py = lax.rem(x + r // NY, NX), lax.rem(y + r % NY, NY)
        plane.append((px * NY + py, device(px, py, z, c)))
    line = []
    for r in range(1, NZ):
        pz = lax.rem(z + r, NZ)
        line.append((pz, device(x, y, pz, c)))
    other = device(x, y, z, 1 - c)

    def copy(src, dst, stage, target):
        return pltpu.make_async_remote_copy(
            src_ref=src,
            dst_ref=dst,
            send_sem=send.at[stage],
            recv_sem=recv.at[stage],
            device_id=target,
            device_id_type=MESH,
        )

    barrier = pltpu.get_barrier_semaphore()
    partners = [other] + [d for _, d in plane] + [d for _, d in line]
    for target in partners:
        pl.semaphore_signal(barrier, inc=1, device_id=target, device_id_type=MESH)
    own = pltpu.make_async_copy(ens.at[:, :, 0, :], surf.at[c], local_sem)
    own.start()
    pl.semaphore_wait(barrier, len(partners))
    swap = copy(ens.at[:, :, 0, :], surf.at[c], 0, other)
    swap.start()

    span = pl.ds(pl.multiple_of(c * (HB * BLK), BLK), HB * BLK)
    first = st[bi, 0:1, span]
    base_lat = lax.shift_right_logical(first, 11)
    base_lon = lax.shift_right_logical(first, 4) & (NLON - 1)
    east = (base_lon + 1) & (NLON - 1)
    fa, fo = fr[bi, 0:1, span], fr[bi, 1:2, span]
    cells = lax.broadcasted_iota(jnp.int32, (CL, HB * BLK), 0)
    lat = cells + (x * NZ + z) * CL
    w_lat = jnp.where(lat == base_lat, 1.0 - fa, jnp.where(lat == base_lat + 1, fa, 0.0))

    def partial(core):
        lon = cells + (y * NC + core) * CL
        w_lon = jnp.where(lon == base_lon, 1.0 - fo, jnp.where(lon == east, fo, 0.0))
        w = (w_lat[:, None, :] * w_lon[None, :, :]).reshape(CL * CL, HB * BLK)
        s = surf[core].reshape(CL * CL, MEM).T
        s_hi, s_lo = split(s)
        w_hi, w_lo = split(w)
        return mm(s_hi, w_hi) + (mm(s_lo, w_hi) + mm(s_hi, w_lo))

    own.wait()
    mine = partial(c)
    swap.wait_recv()
    total = mine + partial(1 - c)
    for k in range(HB):
        part[k] = total[:, k * BLK : (k + 1) * BLK]

    for r, (pq, target) in enumerate(plane):
        copy(part.at[:, pl.ds(pl.multiple_of(pq * ROWS, ROWS), ROWS), :], got1.at[r], 1, target).start()
    copy(got1, got1, 1, other).wait_recv()
    mine = part[:, pl.ds(pl.multiple_of(q * ROWS, ROWS), ROWS), :]
    for r in range(len(plane)):
        mine = mine + got1[r]
    acc[...] = mine

    half = ROWS * HB // NZ

    def piece(pz):
        return pz // 2, pl.ds(pl.multiple_of((pz % 2) * half, half), half)

    for r, (pz, target) in enumerate(line):
        blk, rows = piece(pz)
        copy(acc.at[blk, rows, :], got2.at[r], 2, target).start()
    copy(got2, got2, 2, other).wait_recv()
    blk, rows = piece(z)
    mine = acc[blk, rows, :]
    for r in range(len(line)):
        mine = mine + got2[r]
    where = (c * HB + blk, pl.ds(pl.multiple_of(q * ROWS + (z % 2) * half, half), half), slice(None))
    out[where] = mine

    for _, target in line:
        copy(out.at[where], out.at[where], 3, target).start()
    copy(got2, got2, 3, other).wait_recv()
    where2 = (pl.ds(c * HB, HB), pl.ds(pl.multiple_of(q * ROWS, ROWS), ROWS), slice(None))
    for _, target in plane:
        copy(out.at[where2], out.at[where2], 4, target).start()
    copy(got1, got1, 4, other).wait_recv()
    last = copy(out.at[pl.ds(c * HB, HB)], out.at[pl.ds(c * HB, HB)], 5, other)
    last.start()
    last.wait_recv()
    swap.wait_send()
    copy(got1, got1, 1, other).wait_send()
    copy(got2, got2, 2, other).wait_send()
    copy(got2, got2, 3, other).wait_send()
    copy(got1, got1, 4, other).wait_send()
    last.wait_send()


def observe(bi, ens, st, fr):
    return pl.pallas_call(
        functools.partial(observe_kernel, bi),
        out_shape=jax.ShapeDtypeStruct((NB, MEM, BLK), F32),
        in_specs=[
            pl.BlockSpec(memory_space=pl.ANY),
            pl.BlockSpec(memory_space=pltpu.VMEM),
            pl.BlockSpec(memory_space=pltpu.VMEM),
        ],
        out_specs=pl.BlockSpec(memory_space=pltpu.VMEM),
        scratch_shapes=[
            pltpu.VMEM((NC, CL, CL, MEM), F32),
            pltpu.VMEM((HB, MEM, BLK), F32),
            pltpu.VMEM((NX * NY - 1, HB, ROWS, BLK), F32),
            pltpu.VMEM((HB, ROWS, BLK), F32),
            pltpu.VMEM((NZ - 1, ROWS * HB // NZ, BLK), F32),
            pltpu.SemaphoreType.DMA,
            pltpu.SemaphoreType.DMA((6,)),
            pltpu.SemaphoreType.DMA((6,)),
        ],
        compiler_params=pltpu.CompilerParams(
            collective_id=bi, has_side_effects=True, vmem_limit_bytes=32 << 20
        ),
        name="observe",
    )(ens, st, fr)


def inverse(m):
    n = m.shape[0]
    row_id = lax.broadcasted_iota(jnp.int32, (n, n), 0)
    col_id = lax.broadcasted_iota(jnp.int32, (n, n), 1)
    for k in range(n):
        inv = 1.0 / m[k : k + 1, k : k + 1]
        row = m[k : k + 1, :] * inv
        col = m[:, k : k + 1]
        swept = m - col * row
        swept = jnp.where(col_id == k, col * inv, swept)
        m = jnp.where(row_id == k, jnp.where(col_id == k, -inv, row), swept)
    return -m


def taper_gc(scaled):
    inner_part = (
        ((-0.25 * scaled + 0.5) * scaled + 0.625) * scaled - 5.0 / 3.0
    ) * scaled * scaled + 1.0
    outer_part = (
        ((((scaled / 12.0 - 0.5) * scaled + 0.625) * scaled + 5.0 / 3.0) * scaled - 5.0) * scaled
        + 4.0
        - 2.0 / (3.0 * jnp.maximum(scaled, 1.0))
    )
    return jnp.where(scaled <= 1.0, inner_part, jnp.where(scaled <= 2.0, outer_part, 0.0))


META = 16


def update_kernel(
    bi, ens, observed, st, fr, value, variance, out, anom, packed, chosen, apack, spack, meta
):
    x, y, z, c = place()
    lat0 = ((x * NZ + z) * CL).astype(F32)
    lon0 = ((y * NC + c) * CL).astype(F32)

    var_row = variance[bi : bi + 1, :]
    inv_row = 1.0 / var_row
    for k in range(NB):
        lanes = slice(k * BLK, (k + 1) * BLK)
        block = observed[k]
        mean = jnp.sum(block, axis=0, keepdims=True) / MEM
        block = block - mean
        anom[0:MEM, lanes] = block
        anom[MEM : MEM + 8, lanes] = jnp.broadcast_to(value[bi : bi + 1, lanes] - mean, (8, BLK))
        hi, lo = split(block)
        packed[0:MEM, lanes] = hi
        packed[MEM : 2 * MEM, lanes] = lo
    innovation = anom[MEM : MEM + 1, :]
    gram = mm_nt(anom[0:MEM, :] * inv_row, anom[...], HIGHEST)
    eye = (
        lax.broadcasted_iota(jnp.int32, (MEM, MEM), 0)
        == lax.broadcasted_iota(jnp.int32, (MEM, MEM), 1)
    )
    inv = inverse(gram[:, 0:MEM] + jnp.where(eye, MEM - 1.0, 0.0))
    h = jnp.sum(inv * gram[:, MEM : MEM + 1], axis=0, keepdims=True)
    factor = (0.5 * (MEM - 1.0)) * inv + h

    first = st[bi, 0:1, :]
    obs_lat = lax.shift_right_logical(first, 11).astype(F32) + fr[bi, 0:1, :]
    obs_lon = (lax.shift_right_logical(first, 4) & (NLON - 1)).astype(F32) + fr[bi, 1:2, :]
    half = 0.5 * (CL - 1)
    d_lat = jnp.maximum(jnp.abs(obs_lat - (lat0 + half)) - half, 0.0)
    d_lon = jnp.abs(obs_lon - (lon0 + half))
    d_lon = jnp.maximum(jnp.minimum(d_lon, NLON - d_lon) - half, 0.0)
    reach = 2.0 * CL
    near = jnp.where(d_lat * d_lat + d_lon * d_lon <= reach * reach + 0.5, 1.0, 0.0)
    rows = jnp.concatenate([near[:, k * BLK : (k + 1) * BLK] for k in range(NB)], axis=0)
    before = (
        lax.broadcasted_iota(jnp.int32, (BLK, BLK), 0)
        < lax.broadcasted_iota(jnp.int32, (BLK, BLK), 1)
    )
    rank = mm(rows.astype(BF16), jnp.where(before, 1.0, 0.0).astype(BF16))
    count = mm(rows.astype(BF16), jnp.ones((BLK, BLK), BF16))
    offset = jnp.zeros((1, BLK), F32)
    for k in range(NB):
        chosen[k : k + 1, :] = jnp.where(
            rows[k : k + 1, :] > 0.0, rank[k : k + 1, :] + offset, -1.0
        )
        offset = offset + count[k : k + 1, :]
    chunks = (jnp.sum(near).astype(jnp.int32) + (BLK - 1)) // BLK

    zero = jnp.zeros((1, NOBS), BF16)
    lines = [*split3(obs_lat), *split3(obs_lon), *split3(inv_row), *split3(innovation)]
    packed[2 * MEM :, :] = jnp.concatenate(lines + [zero] * (META - len(lines)), axis=0)

    def gather(chunk, carry):
        slot = lax.broadcasted_iota(jnp.int32, (BLK, BLK), 0).astype(F32) + (chunk * BLK).astype(F32)
        pick = jnp.concatenate(
            [jnp.where(chosen[k : k + 1, :] == slot, 1.0, 0.0).astype(BF16) for k in range(NB)],
            axis=1,
        )
        got = mm_nt(packed[...], pick)
        near_anom = got[0:MEM] + got[MEM : 2 * MEM]

        def line(k):
            r = 2 * MEM + 3 * k
            return got[r : r + 1] + (got[r + 1 : r + 2] + got[r + 2 : r + 3])

        near_spread = (
            line(3) - jnp.dot(factor, near_anom, preferred_element_type=F32, precision=HIGHEST)
        ).T
        for ref, val in ((apack, near_anom), (spack, near_spread)):
            both = jnp.concatenate(split(val), axis=1)
            ref[chunk, 0:MEM, :] = both
            ref[chunk, MEM:, :] = both
        meta[chunk, 0:1, :] = line(0)
        meta[chunk, 1:2, :] = line(1)
        meta[chunk, 2:3, :] = line(2) / (MEM - 1.0)
        return carry

    lax.fori_loop(0, chunks, gather, 0)

    def rows_of(step, carry):
        lats = pl.ds(step * TL, TL)
        state = ens[lats]
        anomaly = state - jnp.mean(state, axis=-1, keepdims=True)
        left = jnp.concatenate(split(anomaly.reshape(TL * CL * DEPTH, MEM)), axis=1)
        out[lats] = state

        def add(chunk, carry):
            lon = lax.broadcasted_iota(jnp.int32, (CL, BLK), 0).astype(F32) + lon0
            lon_diff = jnp.abs(lon - meta[chunk, 1:2, :])
            lon_diff = jnp.minimum(lon_diff, NLON - lon_diff)
            tapers = []
            for i in range(TL):
                lat_diff = (lat0 + (step * TL + i).astype(F32)) - meta[chunk, 0:1, :]
                distance = jnp.sqrt(lat_diff * lat_diff + lon_diff * lon_diff)
                tapers.append(taper_gc(distance / CL) * meta[chunk, 2:3, :])
            taper = jnp.stack(tapers)
            cov = mm(left, apack[chunk])
            cov = (cov[:, 0:BLK] + cov[:, BLK:]).reshape(TL, CL, DEPTH, BLK) * taper[:, :, None, :]
            cov = jnp.concatenate(split(cov.reshape(TL * CL * DEPTH, BLK)), axis=1)
            delta = mm(cov, spack[chunk])
            delta = delta[:, 0:MEM] + delta[:, MEM:]
            out[lats] = out[lats] + delta.reshape(TL, CL, DEPTH, MEM)
            return carry

        return lax.fori_loop(0, chunks, add, carry)

    lax.fori_loop(0, CL // TL, rows_of, 0)


def update(bi, ens, observed, st, fr, value, variance):
    vmem = pl.BlockSpec(memory_space=pltpu.VMEM)
    return pl.pallas_call(
        functools.partial(update_kernel, bi),
        out_shape=jax.ShapeDtypeStruct(ens.shape, F32),
        in_specs=[vmem] * 6,
        out_specs=vmem,
        scratch_shapes=[
            pltpu.VMEM((MEM + 8, NOBS), F32),
            pltpu.VMEM((2 * MEM + META, NOBS), BF16),
            pltpu.VMEM((NB, BLK), F32),
            pltpu.VMEM((NB, 2 * MEM, 2 * BLK), BF16),
            pltpu.VMEM((NB, 2 * BLK, 2 * MEM), BF16),
            pltpu.VMEM((NB, 8, BLK), F32),
        ],
        compiler_params=pltpu.CompilerParams(vmem_limit_bytes=48 << 20),
        name="update",
    )(ens, observed, st, fr, value, variance)


def local(prior, stencil_rows, obs_frac, obs_value, obs_var):
    st = jnp.transpose(stencil_rows, (0, 2, 1))
    fr = jnp.transpose(obs_frac, (0, 2, 1))
    ens = prior
    for bi in range(stencil_rows.shape[0]):
        observed = observe(bi, ens, st, fr)
        ens = update(bi, ens, observed, st, fr, obs_value, obs_var)
    return ens


def solution(mesh):
    placed = (P("lat", "lon", None, None), P(), P(), P(), P())
    return jax.shard_map(
        local, mesh=mesh, in_specs=placed, out_specs=P("lat", "lon", None, None), check_vma=False
    )
```

time: 2000 us -> 108 us (0.05)
  waiting for transfers between devices: 1700 us -> 0 us
  matrix products: 128 us -> 0 us
  Pallas kernels: 0 us -> 105 us
  other arithmetic: 91.4 us -> 0 us
  local copies, waits for them, and re-layouts: 35 us -> 3.08 us
    psum x4 -> x0, waiting for transfers between devices: 1700 us -> none  [the longest x2 1210 us: from_root(): return lax.psum(jnp.where(mine, x, jnp.zeros_like(x)), axis)]
    dot_general x64 -> x0, matrix products: 128 us -> none  [the longest x32 67.3 us: update_level(): jnp.dot(anomaly, obs_anom.T, precision=lax.Precision.HIGHEST)]
    pallas_call x0 -> x4, Pallas kernels: none -> 105 us  [the longest x2 63.1 us: observe(): pl.pallas_call(functools.partial(observe_kernel, bi), out_shape=jax.Shape...]
    reduce_sum x36 -> x0, other arithmetic: 47.9 us -> none  [the longest x32 32.6 us: update_level(): anomaly = level_state - jnp.mean(level_state, axis=-1, keepdims=True)]
    sub x34 -> x0, other arithmetic: 21.8 us -> none  [the longest x32 21.4 us: taper_gc(): ((-0.25 * scaled + 0.5) * scaled + 0.625) * scaled - 5.0 / 3.0]
    gather x2 -> x0, local copies, waits for them, and re-layouts: 21.5 us -> none  [local(): picked = surface[local_idx]]
  transfers between devices with their start and end apart: 4 -> 0, of which waited for: 4 -> 0; matrix products, arithmetic and copies ran while one was open for 0% -> 0% of each run, Pallas kernels for 0% -> 0%
where the time goes in v1:
time: 108 us
  Pallas kernels  105 us (97%)
  local copies, waits for them, and re-layouts  3.08 us (3%)
    pallas_call x2, Pallas kernels, observe(): pl.pallas_call(functools.partial(observe_kernel, bi), out_shape=jax.Shape...  63.1 us
    pallas_call x2, Pallas kernels, update(): pl.pallas_call(functools.partial(update_kernel, bi), out_shape=jax.ShapeD...  41.5 us
    unnamed x14, local copies, waits for them, and re-layouts  3.08 us

profile of v1, /device:TPU:1, one launch (start us, length us, event | category | flops | bytes accessed | tf_op | source)
XLA Modules:
  0.0 107.7 jit_solution(4306237304702246417)
XLA Ops:
  0.0 0.0 copy-start
  0.0 1.6 %copy-done = f32[16,16,16,128]{3,2,1,0:T(8,128)S(1)} copy-done((f32[16,16,16,128]{3,2,1,0:T(8,128)S(1)}, f32[16,16,16,128]{3,2,1,0:T(8,128)}, u32[]{:S(2)}) %copy-start) | copy-done | bytes 2097176
  1.6 0.0 copy-start.2
  1.6 0.8 copy-done.2
  2.4 0.0 copy-start.4
  2.4 0.7 copy-done.4
  3.1 0.0 copy-start.1
  3.1 0.0 copy-start.3
  3.1 0.0 copy-start.5
  3.1 0.0 copy-start.6
  3.1 34.6 %observe.2.observed = f32[8,128,128]{2,1,0:T(8,128)S(1)} custom-call(f32[16,16,16,128]{3,2,1,0:T(8,128)S(1)} %copy-done, s32[2,4,1024]{2,1,0:T(4,128)S(1)} %bitcast.2, f32[2,2,1024]{2,1,0:T(2,128)S(1)} %bitcast.6), custom_call_target="tpu_custom_call" | custom-call | tf_op jit(solution)/shard_map/observe/pallas_call | solution.py:161
  37.7 0.0 copy-done.1
  37.7 0.0 copy-done.3
  37.7 0.0 copy-done.5
  37.8 0.0 copy-done.6
  37.8 20.2 %update.2.ens = f32[16,16,16,128]{3,2,1,0:T(8,128)S(1)} custom-call(f32[16,16,16,128]{3,2,1,0:T(8,128)S(1)} %copy-done.1, f32[8,128,128]{2,1,0:T(8,128)S(1)} %observe.2.observed, s32[2,4,1024]{2,1,0:T(4,128)S(1)} %bitcast.3, f32[2,2,1024]{2,1,0:T(2,128)S(1)} %bitcast.7, f32[2,1024]{1,0:T(2,128)S(1)} %copy-done.5, f32[2,1024]{1,0:T(2,128)S(1)} %copy-done.6), custom_call_target="tpu_custom_call" | custom-call | tf_op jit(solution)/shard_map/update/pallas_call | solution.py:332
  57.9 28.5 %observe.3.observed = f32[8,128,128]{2,1,0:T(8,128)S(1)} custom-call(f32[16,16,16,128]{3,2,1,0:T(8,128)S(1)} %update.2.ens, s32[2,4,1024]{2,1,0:T(4,128)S(1)} %bitcast.4, f32[2,2,1024]{2,1,0:T(2,128)S(1)} %bitcast.8), custom_call_target="tpu_custom_call" | custom-call | tf_op jit(solution)/shard_map/observe/pallas_call | solution.py:161
  86.4 21.3 %update.3 = f32[16,16,16,128]{3,2,1,0:T(8,128)} custom-call(f32[16,16,16,128]{3,2,1,0:T(8,128)S(1)} %update.2.ens, f32[8,128,128]{2,1,0:T(8,128)S(1)} %observe.3.observed, s32[2,4,1024]{2,1,0:T(4,128)S(1)} %bitcast.5, f32[2,2,1024]{2,1,0:T(2,128)S(1)} %bitcast.9, f32[2,1024]{1,0:T(2,128)S(1)} %copy-done.5, f32[2,1024]{1,0:T(2,128)S(1)} %copy-done.6), custom_call_target="tpu_custom_call" | custom-call | tf_op jit(solution)/shard_map/update/pallas_call | solution.py:332
Async XLA Ops:
  0.0 1.6 %copy-start = (f32[16,16,16,128]{3,2,1,0:T(8,128)S(1)}, f32[16,16,16,128]{3,2,1,0:T(8,128)}, u32[]{:S(2)}) copy-start(f32[16,16,16,128]{3,2,1,0:T(8,128)} %ens.3) | copy-start | bytes 6291460
  1.6 0.8 copy-start.2
  2.4 0.7 copy-start.4
  3.1 34.7 %copy-start.1 = (f32[16,16,16,128]{3,2,1,0:T(8,128)S(1)}, f32[16,16,16,128]{3,2,1,0:T(8,128)}, u32[]{:S(2)}) copy-start(f32[16,16,16,128]{3,2,1,0:T(8,128)} %ens.3) | copy-start | bytes 6291460
  3.1 34.7 %copy-start.3 = (s32[2,1024,4]{1,2,0:T(4,128)S(1)}, s32[2,1024,4]{1,2,0:T(4,128)}, u32[]{:S(2)}) copy-start(s32[2,1024,4]{1,2,0:T(4,128)} %param.6) | copy-start | bytes 98308
  3.1 34.7 %copy-start.5 = (f32[2,1024]{1,0:T(2,128)S(1)}, f32[2,1024]{1,0:T(2,128)}, u32[]{:S(2)}) copy-start(f32[2,1024]{1,0:T(2,128)} %value.3) | copy-start | bytes 24580
  3.1 34.7 %copy-start.6 = (f32[2,1024]{1,0:T(2,128)S(1)}, f32[2,1024]{1,0:T(2,128)}, u32[]{:S(2)}) copy-start(f32[2,1024]{1,0:T(2,128)} %variance.3) | copy-start | bytes 24580

commit v2 on v0

v2 whole, which is shorter than its diff:
```python
import functools

import jax
import jax.numpy as jnp
from jax import lax
from jax.experimental import pallas as pl
from jax.experimental.pallas import tpu as pltpu
from jax.sharding import PartitionSpec as P

MESH = pl.DeviceIdType.MESH
F32, BF16 = jnp.float32, jnp.bfloat16
HIGHEST = lax.Precision.HIGHEST
NX, NY, NZ, NC = 4, 4, 8, 2
CL = 16
DEPTH = 16
MEM = 128
NOBS = 1024
NLON = 128
BLK = 128
NB = NOBS // BLK
HB = NB // NC
ROWS = 8
TL = 4
STEPS = 13


def split(v):
    hi = v.astype(BF16)
    return hi, (v - hi.astype(F32)).astype(BF16)


def split3(v):
    hi = v.astype(BF16)
    rest = v - hi.astype(F32)
    mid = rest.astype(BF16)
    return hi, mid, (rest - mid.astype(F32)).astype(BF16)


def mm(a, b):
    return jnp.dot(a, b, preferred_element_type=F32)


def mm_nt(a, b, precision=None):
    return lax.dot_general(
        a, b, (((1,), (1,)), ((), ())), preferred_element_type=F32, precision=precision
    )


def place():
    lat, lon = lax.axis_index("lat"), lax.axis_index("lon")
    return lat // NZ, lon // NC, lat % NZ, lon % NC


def device(x, y, z, c):
    return (x * NZ + z, y * NC + c)


def eye(scale):
    diagonal = lax.broadcasted_iota(jnp.int32, (MEM, MEM), 0) == lax.broadcasted_iota(
        jnp.int32, (MEM, MEM), 1
    )
    return jnp.where(diagonal, scale, 0.0)


def dot(a, b):
    return jnp.dot(a, b, preferred_element_type=F32, precision=HIGHEST)


def inverse_start(m):
    bound = jnp.max(jnp.sum(jnp.abs(m), axis=0, keepdims=True), axis=1, keepdims=True)
    scale = 1.0 / bound
    return jnp.concatenate([eye(1.0) * scale, m * scale], axis=0), (MEM - 1.0) * scale


def inverse_step(xy, low):
    s = jnp.minimum(2.0 / (1.0 + low), 1.95)
    z = eye(2.0) * s - xy[MEM:, :] * (s * s)
    t = s * low
    return dot(xy, z), jnp.minimum(t * (2.0 - t), s * (2.0 - s))


def inverse_finish(m, x):
    return x + dot(x, eye(1.0) - dot(m, x))


def taper_gc(scaled):
    inner_part = (
        ((-0.25 * scaled + 0.5) * scaled + 0.625) * scaled - 5.0 / 3.0
    ) * scaled * scaled + 1.0
    outer_part = (
        ((((scaled / 12.0 - 0.5) * scaled + 0.625) * scaled + 5.0 / 3.0) * scaled - 5.0) * scaled
        + 4.0
        - 2.0 / (3.0 * jnp.maximum(scaled, 1.0))
    )
    return jnp.where(scaled <= 1.0, inner_part, jnp.where(scaled <= 2.0, outer_part, 0.0))


def positions(st, fr, bi, lanes):
    first = st[bi, 0:1, lanes]
    obs_lat = lax.shift_right_logical(first, 11).astype(F32) + fr[bi, 0:1, lanes]
    obs_lon = (lax.shift_right_logical(first, 4) & (NLON - 1)).astype(F32) + fr[bi, 1:2, lanes]
    return obs_lat, obs_lon


def centre(observed, value, bi, anom, packed):
    for k in range(NB):
        lanes = slice(k * BLK, (k + 1) * BLK)
        block = observed[k]
        mean = jnp.sum(block, axis=0, keepdims=True) / MEM
        block = block - mean
        anom[0:MEM, lanes] = block
        anom[MEM : MEM + 8, lanes] = jnp.broadcast_to(value[bi : bi + 1, lanes] - mean, (8, BLK))
        hi, lo = split(block)
        packed[0:MEM, lanes] = hi
        packed[MEM : 2 * MEM, lanes] = lo


def normal(anom, inv_row):
    gram = mm_nt(anom[0:MEM, :] * inv_row, anom[...], HIGHEST)
    return gram[:, 0:MEM] + eye(MEM - 1.0), gram[:, MEM : MEM + 1]


def spread_factor(inv, g):
    return (0.5 * (MEM - 1.0)) * inv + jnp.sum(inv * g, axis=0, keepdims=True)


def observe_kernel(
    ens, st_in, fr_in, value_in, var_in, out0, out1, factor_out,
    st, fr, value, variance, surf, part, got1, got2, anom, packed, taper, load, send, recv,
):
    x, y, z, c = place()
    q = x * NY + y
    plane = []
    for r in range(1, NX * NY):
        px, py = lax.rem(x + r // NY, NX), lax.rem(y + r % NY, NY)
        plane.append((px * NY + py, device(px, py, z, c)))
    line = [device(x, y, lax.rem(z + r, NZ), c) for r in range(1, NZ)]
    other = device(x, y, z, 1 - c)

    def copy(src, dst, bi, stage, target):
        return pltpu.make_async_remote_copy(
            src_ref=src,
            dst_ref=dst,
            send_sem=send.at[bi, stage],
            recv_sem=recv.at[bi, stage],
            device_id=target,
            device_id_type=MESH,
        )

    loads = [
        pltpu.make_async_copy(ens.at[:, :, 0, :], surf.at[0, c], load.at[0]),
        pltpu.make_async_copy(st_in, st, load.at[1]),
        pltpu.make_async_copy(fr_in, fr, load.at[2]),
        pltpu.make_async_copy(value_in, value, load.at[3]),
        pltpu.make_async_copy(var_in, variance, load.at[4]),
    ]
    for one in loads:
        one.start()
    barrier = pltpu.get_barrier_semaphore()
    partners = [other] + [d for _, d in plane] + line
    for target in partners:
        pl.semaphore_signal(barrier, inc=1, device_id=target, device_id_type=MESH)
    for one in loads:
        one.wait()

    span = pl.ds(pl.multiple_of(c * (HB * BLK), BLK), HB * BLK)
    cells = lax.broadcasted_iota(jnp.int32, (CL, HB * BLK), 0)
    members = pl.ds(pl.multiple_of(q * ROWS, ROWS), ROWS)
    blocks = pl.ds(c * HB, HB)

    def partial(bi, core):
        first = st[bi, 0:1, span]
        base_lat = lax.shift_right_logical(first, 11)
        base_lon = lax.shift_right_logical(first, 4) & (NLON - 1)
        east = (base_lon + 1) & (NLON - 1)
        fa, fo = fr[bi, 0:1, span], fr[bi, 1:2, span]
        lat = cells + (x * NZ + z) * CL
        lon = cells + (y * NC + core) * CL
        w_lat = jnp.where(lat == base_lat, 1.0 - fa, jnp.where(lat == base_lat + 1, fa, 0.0))
        w_lon = jnp.where(lon == base_lon, 1.0 - fo, jnp.where(lon == east, fo, 0.0))
        w = (w_lat[:, None, :] * w_lon[None, :, :]).reshape(CL * CL, HB * BLK)
        s_hi, s_lo = split(surf[bi, core].reshape(CL * CL, MEM).T)
        w_hi, w_lo = split(w)
        return mm(s_hi, w_hi) + (mm(s_lo, w_hi) + mm(s_hi, w_lo))

    def total(bi, out):
        swap = copy(surf.at[bi, c], surf.at[bi, c], bi, 0, other)
        swap.start()
        mine = partial(bi, c)
        swap.wait_recv()
        mine = mine + partial(bi, 1 - c)
        for k in range(HB):
            part[bi, k] = mine[:, k * BLK : (k + 1) * BLK]
        for r, (pq, target) in enumerate(plane):
            rows = pl.ds(pl.multiple_of(pq * ROWS, ROWS), ROWS)
            copy(part.at[bi, :, rows, :], got1.at[bi, r], bi, 1, target).start()
        if bi == 0:
            tapers()
        copy(got1.at[bi], got1.at[bi], bi, 1, other).wait_recv()
        mine = part[bi, :, members, :]
        for r in range(len(plane)):
            mine = mine + got1[bi, r]
        got2[bi, z] = mine
        for target in line:
            copy(got2.at[bi, z], got2.at[bi, z], bi, 2, target).start()
        seven = got2.at[bi, pl.ds(0, NZ - 1)]
        copy(seven, seven, bi, 2, other).wait_recv()
        mine = got2[bi, 0]
        for r in range(1, NZ):
            mine = mine + got2[bi, r]
        out[blocks, members, :] = mine
        own = out.at[blocks, members, :]
        for _, target in plane:
            copy(own, own, bi, 3, target).start()
        copy(got1.at[bi], got1.at[bi], bi, 3, other).wait_recv()
        half = out.at[blocks]
        copy(half, half, bi, 4, other).start()
        copy(half, half, bi, 4, other).wait_recv()

    def tapers():
        lon0 = ((y * NC + c) * CL).astype(F32)
        lat0 = ((x * NZ + z) * CL).astype(F32)
        for k in range(NB):
            lanes = slice(k * BLK, (k + 1) * BLK)
            obs_lat, obs_lon = positions(st, fr, 0, lanes)
            weight = 1.0 / (variance[0:1, lanes] * (MEM - 1.0))
            lon = lax.broadcasted_iota(jnp.int32, (CL, BLK), 0).astype(F32) + lon0
            lon_diff = jnp.abs(lon - obs_lon)
            lon_diff = jnp.minimum(lon_diff, NLON - lon_diff)
            lon_diff = lon_diff * lon_diff

            def one(i, carry):
                lat_diff = (lat0 + lax.convert_element_type(i, F32)) - obs_lat
                distance = jnp.sqrt(lat_diff * lat_diff + lon_diff)
                rows = pl.ds(pl.multiple_of(i * CL, CL), CL)
                taper[rows, lanes] = taper_gc(distance / CL) * weight
                return carry

            lax.fori_loop(0, CL, one, 0)

    pl.semaphore_wait(barrier, len(partners))
    total(0, out0)

    centre(out0, value, 0, anom, packed)
    m, g = normal(anom, 1.0 / variance[0:1, :])
    xy, low = inverse_start(m)
    for _ in range(STEPS):
        xy, low = inverse_step(xy, low)
    factor = spread_factor(inverse_finish(m, xy[0:MEM, :]), g)
    factor_out[...] = factor

    surface = surf[0, c].reshape(CL * CL, MEM)
    a_hi, a_lo = split(surface - jnp.mean(surface, axis=-1, keepdims=True))
    cov = mm(a_hi, packed[0:MEM, :]) + (
        mm(a_lo, packed[0:MEM, :]) + mm(a_hi, packed[MEM : 2 * MEM, :])
    )
    cov_hi, cov_lo = split(cov * taper[...])
    s_hi, s_lo = split(anom[MEM : MEM + 1, :] - dot(factor, anom[0:MEM, :]))
    delta = mm_nt(cov_hi, s_hi) + (mm_nt(cov_lo, s_hi) + mm_nt(cov_hi, s_lo))
    surf[1, c] = (surface + delta).reshape(CL, CL, MEM)

    total(1, out1)

    for bi, out in ((0, out0), (1, out1)):
        copy(surf.at[bi, c], surf.at[bi, c], bi, 0, other).wait_send()
        copy(got1.at[bi], got1.at[bi], bi, 1, other).wait_send()
        seven = got2.at[bi, pl.ds(0, NZ - 1)]
        copy(seven, seven, bi, 2, other).wait_send()
        copy(got1.at[bi], got1.at[bi], bi, 3, other).wait_send()
        copy(out.at[blocks], out.at[blocks], bi, 4, other).wait_send()


def observe(ens, st, fr, value, variance):
    vmem = pl.BlockSpec(memory_space=pltpu.VMEM)
    block = jax.ShapeDtypeStruct((NB, MEM, BLK), F32)
    batches = st.shape[0]
    return pl.pallas_call(
        observe_kernel,
        out_shape=(block, block, jax.ShapeDtypeStruct((MEM, MEM), F32)),
        in_specs=[pl.BlockSpec(memory_space=pltpu.HBM)] * 5,
        out_specs=(vmem, vmem, vmem),
        scratch_shapes=[
            pltpu.VMEM(st.shape, jnp.int32),
            pltpu.VMEM(fr.shape, F32),
            pltpu.VMEM(value.shape, F32),
            pltpu.VMEM(variance.shape, F32),
            pltpu.VMEM((batches, NC, CL, CL, MEM), F32),
            pltpu.VMEM((batches, HB, MEM, BLK), F32),
            pltpu.VMEM((batches, NX * NY - 1, HB, ROWS, BLK), F32),
            pltpu.VMEM((batches, NZ, HB, ROWS, BLK), F32),
            pltpu.VMEM((MEM + 8, NOBS), F32),
            pltpu.VMEM((2 * MEM, NOBS), BF16),
            pltpu.VMEM((CL * CL, NOBS), F32),
            pltpu.SemaphoreType.DMA((5,)),
            pltpu.SemaphoreType.DMA((batches, 5)),
            pltpu.SemaphoreType.DMA((batches, 5)),
        ],
        compiler_params=pltpu.CompilerParams(
            collective_id=0, has_side_effects=True, vmem_limit_bytes=32 << 20
        ),
        name="observe",
    )(ens, st, fr, value, variance)


META = 16


def update_kernel(
    ens, observed0, observed1, factor0, st, fr, value, variance, out,
    anom, packed, chosen, apack, spack, meta, work,
):
    x, y, z, c = place()
    lat0 = ((x * NZ + z) * CL).astype(F32)
    lon0 = ((y * NC + c) * CL).astype(F32)
    all_obs = slice(0, NOBS)

    def select(bi, observed, solve):
        centre(observed, value, bi, anom, packed)
        inv_row = 1.0 / variance[bi : bi + 1, :]
        factor = solve(inv_row)
        obs_lat, obs_lon = positions(st, fr, bi, all_obs)
        half = 0.5 * (CL - 1)
        d_lat = jnp.maximum(jnp.abs(obs_lat - (lat0 + half)) - half, 0.0)
        d_lon = jnp.abs(obs_lon - (lon0 + half))
        d_lon = jnp.maximum(jnp.minimum(d_lon, NLON - d_lon) - half, 0.0)
        reach = 2.0 * CL
        near = jnp.where(d_lat * d_lat + d_lon * d_lon <= reach * reach + 0.5, 1.0, 0.0)
        rows = jnp.concatenate([near[:, k * BLK : (k + 1) * BLK] for k in range(NB)], axis=0)
        before = lax.broadcasted_iota(jnp.int32, (BLK, BLK), 0) < lax.broadcasted_iota(
            jnp.int32, (BLK, BLK), 1
        )
        rank = mm(rows.astype(BF16), jnp.where(before, 1.0, 0.0).astype(BF16))
        count = mm(rows.astype(BF16), jnp.ones((BLK, BLK), BF16))
        offset = jnp.zeros((1, BLK), F32)
        for k in range(NB):
            chosen[k : k + 1, :] = jnp.where(
                rows[k : k + 1, :] > 0.0, rank[k : k + 1, :] + offset, -1.0
            )
            offset = offset + count[k : k + 1, :]
        chunks = (jnp.sum(near).astype(jnp.int32) + (BLK - 1)) // BLK

        zero = jnp.zeros((1, NOBS), BF16)
        lines = [
            *split3(obs_lat), *split3(obs_lon), *split3(inv_row), *split3(anom[MEM : MEM + 1, :])
        ]
        packed[2 * MEM :, :] = jnp.concatenate(lines + [zero] * (META - len(lines)), axis=0)

        def gather(chunk, carry):
            slot = (lax.broadcasted_iota(jnp.int32, (BLK, BLK), 0) + chunk * BLK).astype(F32)
            pick = jnp.concatenate(
                [
                    jnp.where(chosen[k : k + 1, :] == slot, 1.0, 0.0).astype(BF16)
                    for k in range(NB)
                ],
                axis=1,
            )
            got = mm_nt(packed[...], pick)
            near_anom = got[0:MEM] + got[MEM : 2 * MEM]

            def line(k):
                r = 2 * MEM + 3 * k
                return got[r : r + 1] + (got[r + 1 : r + 2] + got[r + 2 : r + 3])

            near_spread = (line(3) - dot(factor, near_anom)).T
            for ref, val in ((apack, near_anom), (spack, near_spread)):
                both = jnp.concatenate(split(val), axis=1)
                ref[bi, chunk, 0:MEM, :] = both
                ref[bi, chunk, MEM:, :] = both
            meta[bi, chunk, 0:1, :] = line(0)
            meta[bi, chunk, 1:2, :] = line(1)
            meta[bi, chunk, 2:3, :] = line(2) / (MEM - 1.0)
            return carry

        lax.fori_loop(0, chunks, gather, 0)
        return chunks

    def solve(inv_row):
        m, g = normal(anom, inv_row)
        xy, low = inverse_start(m)
        work[...] = xy

        def step(low):
            xy, low = inverse_step(work[...], jnp.full((1, 1), low, F32))
            work[...] = xy
            return low[0, 0]

        lax.while_loop(lambda low: low < 0.999, step, low[0, 0])
        return spread_factor(inverse_finish(m, work[0:MEM, :]), g)

    counts = (
        select(0, observed0, lambda inv_row: factor0[...]),
        select(1, observed1, solve),
    )

    def rows_of(step, carry):
        lats = pl.ds(step * TL, TL)
        out[lats] = ens[lats]
        for bi, chunks in enumerate(counts):
            state = out[lats]
            anomaly = state - jnp.mean(state, axis=-1, keepdims=True)
            left = jnp.concatenate(split(anomaly.reshape(TL * CL * DEPTH, MEM)), axis=1)

            def add(chunk, carry):
                lon = lax.broadcasted_iota(jnp.int32, (CL, BLK), 0).astype(F32) + lon0
                lon_diff = jnp.abs(lon - meta[bi, chunk, 1:2, :])
                lon_diff = jnp.minimum(lon_diff, NLON - lon_diff)
                tapers = []
                for i in range(TL):
                    lat_diff = (lat0 + (step * TL + i).astype(F32)) - meta[bi, chunk, 0:1, :]
                    distance = jnp.sqrt(lat_diff * lat_diff + lon_diff * lon_diff)
                    tapers.append(taper_gc(distance / CL) * meta[bi, chunk, 2:3, :])
                taper = jnp.stack(tapers)
                cov = mm(left, apack[bi, chunk])
                cov = (cov[:, 0:BLK] + cov[:, BLK:]).reshape(TL, CL, DEPTH, BLK)
                cov = (cov * taper[:, :, None, :]).reshape(TL * CL * DEPTH, BLK)
                delta = mm(jnp.concatenate(split(cov), axis=1), spack[bi, chunk])
                delta = delta[:, 0:MEM] + delta[:, MEM:]
                out[lats] = out[lats] + delta.reshape(TL, CL, DEPTH, MEM)
                return carry

            lax.fori_loop(0, chunks, add, 0)
        return carry

    lax.fori_loop(0, CL // TL, rows_of, 0)


def update(ens, observed0, observed1, factor0, st, fr, value, variance):
    vmem = pl.BlockSpec(memory_space=pltpu.VMEM)
    batches = st.shape[0]
    return pl.pallas_call(
        update_kernel,
        out_shape=jax.ShapeDtypeStruct(ens.shape, F32),
        in_specs=[vmem] * 8,
        out_specs=vmem,
        scratch_shapes=[
            pltpu.VMEM((MEM + 8, NOBS), F32),
            pltpu.VMEM((2 * MEM + META, NOBS), BF16),
            pltpu.VMEM((NB, BLK), F32),
            pltpu.VMEM((batches, NB, 2 * MEM, 2 * BLK), BF16),
            pltpu.VMEM((batches, NB, 2 * BLK, 2 * MEM), BF16),
            pltpu.VMEM((batches, NB, 8, BLK), F32),
            pltpu.VMEM((2 * MEM, MEM), F32),
        ],
        compiler_params=pltpu.CompilerParams(vmem_limit_bytes=48 << 20),
        name="update",
    )(ens, observed0, observed1, factor0, st, fr, value, variance)


def local(prior, stencil_rows, obs_frac, obs_value, obs_var):
    st = jnp.transpose(stencil_rows, (0, 2, 1))
    fr = jnp.transpose(obs_frac, (0, 2, 1))
    observed0, observed1, factor0 = observe(prior, st, fr, obs_value, obs_var)
    return update(prior, observed0, observed1, factor0, st, fr, obs_value, obs_var)


def solution(mesh):
    placed = (P("lat", "lon", None, None), P(), P(), P(), P())
    return jax.shard_map(
        local, mesh=mesh, in_specs=placed, out_specs=P("lat", "lon", None, None), check_vma=False
    )
```

time: 2000 us -> 76.6 us (0.04)
  waiting for transfers between devices: 1700 us -> 0 us
  matrix products: 128 us -> 0 us
  other arithmetic: 91.4 us -> 0 us
  Pallas kernels: 0 us -> 71.8 us
  local copies, waits for them, and re-layouts: 35 us -> 4.47 us
    psum x4 -> x0, waiting for transfers between devices: 1700 us -> none  [the longest x2 1210 us: from_root(): return lax.psum(jnp.where(mine, x, jnp.zeros_like(x)), axis)]
    dot_general x64 -> x0, matrix products: 128 us -> none  [the longest x32 67.3 us: update_level(): jnp.dot(anomaly, obs_anom.T, precision=lax.Precision.HIGHEST)]
    pallas_call x0 -> x2, Pallas kernels: none -> 71.8 us  [the longest x1 59.5 us: observe(): pl.pallas_call(observe_kernel, out_shape=(block, block, jax.ShapeDtypeStr...]
    reduce_sum x36 -> x0, other arithmetic: 47.9 us -> none  [the longest x32 32.6 us: update_level(): anomaly = level_state - jnp.mean(level_state, axis=-1, keepdims=True)]
    sub x34 -> x0, other arithmetic: 21.8 us -> none  [the longest x32 21.4 us: taper_gc(): ((-0.25 * scaled + 0.5) * scaled + 0.625) * scaled - 5.0 / 3.0]
    gather x2 -> x0, local copies, waits for them, and re-layouts: 21.5 us -> none  [local(): picked = surface[local_idx]]
  transfers between devices with their start and end apart: 4 -> 0, of which waited for: 4 -> 0; matrix products, arithmetic and copies ran while one was open for 0% -> 0% of each run, Pallas kernels for 0% -> 0%
where the time goes in v2:
time: 76.6 us; the launch traced here: 76.3 us
  Pallas kernels  71.8 us (94%)
  local copies, waits for them, and re-layouts  4.47 us (6%)
    pallas_call x1, Pallas kernels, observe(): pl.pallas_call(observe_kernel, out_shape=(block, block, jax.ShapeDtypeStr...  59.5 us
    pallas_call x1, Pallas kernels, update(): pl.pallas_call(update_kernel, out_shape=jax.ShapeDtypeStruct(ens.shape, F...  12.3 us
    unnamed x18, local copies, waits for them, and re-layouts  4.47 us

profile of v2, /device:TPU:1, one launch (start us, length us, event | category | flops | bytes accessed | tf_op | source)
XLA Modules:
  0.0 76.3 jit_solution(15830408268871088726)
XLA Ops:
  0.0 0.0 copy-start
  0.0 1.6 %copy-done = f32[16,16,16,128]{3,2,1,0:T(8,128)S(1)} copy-done((f32[16,16,16,128]{3,2,1,0:T(8,128)S(1)}, f32[16,16,16,128]{3,2,1,0:T(8,128)}, u32[]{:S(2)}) %copy-start) | copy-done | bytes 2097176
  1.6 0.0 copy-start.2
  1.6 0.8 copy-done.2
  2.4 0.0 copy-start.4
  2.4 0.7 copy-done.4
  3.1 0.0 copy-start.6
  3.1 0.7 copy-done.6
  3.8 0.0 copy-start.8
  3.8 0.7 copy-done.8
  4.5 0.0 copy-start.1
  4.5 0.0 copy-start.3
  4.5 0.0 copy-start.5
  4.5 0.0 copy-start.7
  4.5 59.5 %observe.1 = (f32[8,128,128]{2,1,0:T(8,128)S(1)}, f32[8,128,128]{2,1,0:T(8,128)S(1)}, f32[128,128]{1,0:T(8,128)S(1)}) custom-call(f32[16,16,16,128]{3,2,1,0:T(8,128)S(1)} %copy-done, s32[2,4,1024]{2,1,0:T(4,128)S(1)} %bitcast.2, f32[2,2,1024]{2,1,0:T(2,128)S(1)} %bitcast.4, f32[2,1024]{1,0:T(2,128)S(1)} %copy-done.6, f32[2,1024]{1,0:T(2,128)S(1)} %copy-done.8), custom_call_target="tpu_custom_call" | custom-call | tf_op jit(solution)/shard_map/observe/pallas_call | solution.py:277
  64.0 0.0 copy-done.1
  64.0 0.0 copy-done.3
  64.0 0.0 copy-done.5
  64.0 0.0 copy-done.7
  64.0 12.3 %update.1 = f32[16,16,16,128]{3,2,1,0:T(8,128)} custom-call(f32[16,16,16,128]{3,2,1,0:T(8,128)S(1)} %copy-done.1, f32[8,128,128]{2,1,0:T(8,128)S(1)} %get-tuple-element.8.observed0, f32[8,128,128]{2,1,0:T(8,128)S(1)} %get-tuple-element.9.observed1, f32[128,128]{1,0:T(8,128)S(1)} %get-tuple-element.10.factor0, s32[2,4,1024]{2,1,0:T(4,128)S(1)} %bitcast.3, ...), custom_call_target="tpu_custom_call" | custom-call | tf_op jit(solution)/shard_map/update/pallas_call | solution.py:430
Async XLA Ops:
  0.0 1.6 %copy-start = (f32[16,16,16,128]{3,2,1,0:T(8,128)S(1)}, f32[16,16,16,128]{3,2,1,0:T(8,128)}, u32[]{:S(2)}) copy-start(f32[16,16,16,128]{3,2,1,0:T(8,128)} %ens.3) | copy-start | bytes 6291460
  1.6 0.8 copy-start.2
  2.4 0.7 copy-start.4
  3.1 0.7 copy-start.6
  3.8 0.7 copy-start.8
  4.5 59.5 %copy-start.1 = (f32[16,16,16,128]{3,2,1,0:T(8,128)S(1)}, f32[16,16,16,128]{3,2,1,0:T(8,128)}, u32[]{:S(2)}) copy-start(f32[16,16,16,128]{3,2,1,0:T(8,128)} %ens.3) | copy-start | bytes 6291460
  4.5 59.5 %copy-start.3 = (s32[2,1024,4]{1,2,0:T(4,128)S(1)}, s32[2,1024,4]{1,2,0:T(4,128)}, u32[]{:S(2)}) copy-start(s32[2,1024,4]{1,2,0:T(4,128)} %param.6) | copy-start | bytes 98308
  4.5 59.5 %copy-start.5 = (f32[2,1024,2]{1,2,0:T(2,128)S(1)}, f32[2,1024,2]{1,2,0:T(2,128)}, u32[]{:S(2)}) copy-start(f32[2,1024,2]{1,2,0:T(2,128)} %param.7) | copy-start | bytes 49156
  4.5 59.5 %copy-start.7 = (f32[2,1024]{1,0:T(2,128)S(1)}, f32[2,1024]{1,0:T(2,128)}, u32[]{:S(2)}) copy-start(f32[2,1024]{1,0:T(2,128)} %value.1) | copy-start | bytes 24580

commit v3 on v2

v3 whole, which is shorter than its diff:
```python
import functools

import jax
import jax.numpy as jnp
from jax import lax
from jax.experimental import pallas as pl
from jax.experimental.pallas import tpu as pltpu
from jax.sharding import PartitionSpec as P

MESH = pl.DeviceIdType.MESH
F32, BF16 = jnp.float32, jnp.bfloat16
HIGHEST = lax.Precision.HIGHEST
NX, NY, NZ, NC = 4, 4, 8, 2
CL = 16
DEPTH = 16
MEM = 128
NOBS = 1024
NLON = 128
BLK = 128
NB = NOBS // BLK
HB = NB // NC
ROWS = 8
TL = 4
EXACT, PACKED = 4, 7
META = 16


def split(v):
    hi = v.astype(BF16)
    return hi, (v - hi.astype(F32)).astype(BF16)


def split3(v):
    hi = v.astype(BF16)
    rest = v - hi.astype(F32)
    mid = rest.astype(BF16)
    return hi, mid, (rest - mid.astype(F32)).astype(BF16)


def mm(a, b):
    return jnp.dot(a, b, preferred_element_type=F32)


def mm_nt(a, b, precision=None):
    return lax.dot_general(
        a, b, (((1,), (1,)), ((), ())), preferred_element_type=F32, precision=precision
    )


def place():
    lat, lon = lax.axis_index("lat"), lax.axis_index("lon")
    return lat // NZ, lon // NC, lat % NZ, lon % NC


def device(x, y, z, c):
    return (x * NZ + z, y * NC + c)


def eye(scale):
    diagonal = lax.broadcasted_iota(jnp.int32, (MEM, MEM), 0) == lax.broadcasted_iota(
        jnp.int32, (MEM, MEM), 1
    )
    return jnp.where(diagonal, scale, 0.0)


def dot(a, b):
    return jnp.dot(a, b, preferred_element_type=F32, precision=HIGHEST)


def inverse_start(m):
    bound = jnp.max(jnp.sum(jnp.abs(m), axis=0, keepdims=True), axis=1, keepdims=True)
    scale = 1.0 / bound
    return jnp.concatenate([eye(1.0) * scale, m * scale], axis=0), (MEM - 1.0) * scale


def pack_left(v):
    return jnp.concatenate(split(v), axis=1)


def pack_right(v):
    both = jnp.concatenate(split(v), axis=1)
    return jnp.concatenate([both, both], axis=0)


def packed_dot(left, right):
    both = mm(left, right)
    n = both.shape[1] // 2
    return both[:, 0:n] + both[:, n:]


def inverse_step(xy, low, exact):
    s = jnp.minimum(2.0 / (1.0 + low), 1.95)
    z = eye(2.0) * s - xy[MEM:, :] * (s * s)
    t = s * low
    low = jnp.minimum(t * (2.0 - t), s * (2.0 - s))
    return (dot(xy, z) if exact else packed_dot(pack_left(xy), pack_right(z))), low


def inverse_finish(m, x):
    return x + dot(x, eye(1.0) - dot(m, x))


def taper_gc(scaled):
    inner_part = (
        ((-0.25 * scaled + 0.5) * scaled + 0.625) * scaled - 5.0 / 3.0
    ) * scaled * scaled + 1.0
    outer_part = (
        ((((scaled / 12.0 - 0.5) * scaled + 0.625) * scaled + 5.0 / 3.0) * scaled - 5.0) * scaled
        + 4.0
        - 2.0 / (3.0 * jnp.maximum(scaled, 1.0))
    )
    return jnp.where(scaled <= 1.0, inner_part, jnp.where(scaled <= 2.0, outer_part, 0.0))


def positions(st, fr, bi, lanes):
    first = st[bi, 0:1, lanes]
    obs_lat = lax.shift_right_logical(first, 11).astype(F32) + fr[bi, 0:1, lanes]
    obs_lon = (lax.shift_right_logical(first, 4) & (NLON - 1)).astype(F32) + fr[bi, 1:2, lanes]
    return obs_lat, obs_lon


def meta_lines(st, fr, variance, bi, lanes, width, innovation):
    obs_lat, obs_lon = positions(st, fr, bi, lanes)
    weight = 1.0 / variance[bi : bi + 1, lanes]
    lines = [*split3(obs_lat), *split3(obs_lon), *split3(weight), *split3(innovation)]
    zero = jnp.zeros((META - len(lines), width), BF16)
    return jnp.concatenate(lines + [zero], axis=0)


def join(got, row):
    return got[row : row + 1] + (got[row + 1 : row + 2] + got[row + 2 : row + 3])


def lon_distance(lon0, obs_lon):
    lon = lax.broadcasted_iota(jnp.int32, (CL, BLK), 0).astype(F32) + lon0
    lon_diff = jnp.abs(lon - obs_lon)
    lon_diff = jnp.minimum(lon_diff, NLON - lon_diff)
    return lon_diff * lon_diff


def lat_taper(lat, obs_lat, lon_diff, weight):
    lat_diff = lat - obs_lat
    return taper_gc(jnp.sqrt(lat_diff * lat_diff + lon_diff) / CL) * weight


def spread_factor(inv, g):
    return (0.5 * (MEM - 1.0)) * inv + jnp.sum(inv * g, axis=0, keepdims=True)


def one_hot(chosen, chunk):
    slot = (lax.broadcasted_iota(jnp.int32, (BLK, BLK), 0) + chunk * BLK).astype(F32)
    return jnp.concatenate(
        [jnp.where(chosen[k : k + 1, :] == slot, 1.0, 0.0).astype(BF16) for k in range(NB)],
        axis=1,
    )


def gather(packed, pick, factor):
    got = mm_nt(packed, pick)
    near_anom = got[0:MEM] + got[MEM : 2 * MEM]
    lines = got[2 * MEM :]
    near_spread = (join(lines, 9) - dot(factor, near_anom)).T
    return pack_right(near_anom), pack_right(near_spread), lines


def increment(state, apack, spack, taper):
    rows = state.shape[0] * CL * DEPTH
    anomaly = state - jnp.mean(state, axis=-1, keepdims=True)
    cov = packed_dot(pack_left(anomaly.reshape(rows, MEM)), apack)
    cov = cov.reshape(state.shape[0], CL, DEPTH, BLK) * taper[:, :, None, :]
    return packed_dot(pack_left(cov.reshape(rows, BLK)), spack).reshape(state.shape)


def observe_kernel(
    ens_in, st_in, fr_in, value_in, var_in,
    ens, packed, chosen, pick1, taper1, gram_out, factor_out,
    state, st, fr, value, variance, surf, part, got1, got2, observed, anom, taper, pick0, taper0,
    apack, spack, load, send, recv,
):
    x, y, z, c = place()
    q = x * NY + y
    lat0 = ((x * NZ + z) * CL).astype(F32)
    lon0 = ((y * NC + c) * CL).astype(F32)
    plane = []
    for r in range(1, NX * NY):
        px, py = lax.rem(x + r // NY, NX), lax.rem(y + r % NY, NY)
        plane.append((px * NY + py, device(px, py, z, c)))
    line = [device(x, y, lax.rem(z + r, NZ), c) for r in range(1, NZ)]
    other = device(x, y, z, 1 - c)

    def copy(src, dst, bi, stage, target):
        return pltpu.make_async_remote_copy(
            src_ref=src,
            dst_ref=dst,
            send_sem=send.at[bi, stage],
            recv_sem=recv.at[bi, stage],
            device_id=target,
            device_id_type=MESH,
        )

    barrier = pltpu.get_barrier_semaphore()
    partners = [other] + [d for _, d in plane] + line
    loads = [
        pltpu.make_async_copy(ens_in.at[:, :, 0, :], surf.at[0, c], load.at[0]),
        pltpu.make_async_copy(st_in, st, load.at[1]),
        pltpu.make_async_copy(fr_in, fr, load.at[2]),
        pltpu.make_async_copy(value_in, value, load.at[3]),
        pltpu.make_async_copy(var_in, variance, load.at[4]),
        pltpu.make_async_copy(ens_in, state, load.at[5]),
    ]
    for one in loads:
        one.start()
    for target in partners:
        pl.semaphore_signal(barrier, inc=1, device_id=target, device_id_type=MESH)
    for one in loads[:-1]:
        one.wait()

    def span_of(core):
        return pl.ds(pl.multiple_of(core * (HB * BLK), BLK), HB * BLK)

    span = span_of(c)
    cells = lax.broadcasted_iota(jnp.int32, (CL, HB * BLK), 0)
    members = pl.ds(pl.multiple_of(q * ROWS, ROWS), ROWS)
    blocks = pl.ds(c * HB, HB)

    def partial(bi, core):
        first = st[bi, 0:1, span]
        base_lat = lax.shift_right_logical(first, 11)
        base_lon = lax.shift_right_logical(first, 4) & (NLON - 1)
        east = (base_lon + 1) & (NLON - 1)
        fa, fo = fr[bi, 0:1, span], fr[bi, 1:2, span]
        lat = cells + (x * NZ + z) * CL
        lon = cells + (y * NC + core) * CL
        w_lat = jnp.where(lat == base_lat, 1.0 - fa, jnp.where(lat == base_lat + 1, fa, 0.0))
        w_lon = jnp.where(lon == base_lon, 1.0 - fo, jnp.where(lon == east, fo, 0.0))
        w = (w_lat[:, None, :] * w_lon[None, :, :]).reshape(CL * CL, HB * BLK)
        s_hi, s_lo = split(surf[bi, core].reshape(CL * CL, MEM).T)
        w_hi, w_lo = split(w)
        return mm(s_hi, w_hi) + (mm(s_lo, w_hi) + mm(s_hi, w_lo))

    def tapers():
        for k in range(NB):
            lanes = slice(k * BLK, (k + 1) * BLK)
            obs_lat, obs_lon = positions(st, fr, 0, lanes)
            weight = 1.0 / (variance[0:1, lanes] * (MEM - 1.0))
            lon_diff = lon_distance(lon0, obs_lon)

            def one(i, carry):
                rows = pl.ds(pl.multiple_of(i * CL, CL), CL)
                lat = lat0 + lax.convert_element_type(i, F32)
                taper[rows, lanes] = lat_taper(lat, obs_lat, lon_diff, weight)
                return carry

            lax.fori_loop(0, CL, one, 0)

    def select(bi, pick, near_taper):
        obs_lat, obs_lon = positions(st, fr, bi, slice(0, NOBS))
        half = 0.5 * (CL - 1)
        d_lat = jnp.maximum(jnp.abs(obs_lat - (lat0 + half)) - half, 0.0)
        d_lon = jnp.abs(obs_lon - (lon0 + half))
        d_lon = jnp.maximum(jnp.minimum(d_lon, NLON - d_lon) - half, 0.0)
        reach = 2.0 * CL
        near = jnp.where(d_lat * d_lat + d_lon * d_lon <= reach * reach + 0.5, 1.0, 0.0)
        rows = jnp.concatenate([near[:, k * BLK : (k + 1) * BLK] for k in range(NB)], axis=0)
        before = lax.broadcasted_iota(jnp.int32, (BLK, BLK), 0) < lax.broadcasted_iota(
            jnp.int32, (BLK, BLK), 1
        )
        rank = mm(rows.astype(BF16), jnp.where(before, 1.0, 0.0).astype(BF16))
        count = mm(rows.astype(BF16), jnp.ones((BLK, BLK), BF16))
        offset = jnp.zeros((1, BLK), F32)
        for k in range(NB):
            chosen[bi, k : k + 1, :] = jnp.where(
                rows[k : k + 1, :] > 0.0, rank[k : k + 1, :] + offset, -1.0
            )
            offset = offset + count[k : k + 1, :]
        pick[...] = one_hot(chosen[bi], 0)
        lines = meta_lines(st, fr, variance, bi, slice(0, NOBS), NOBS, jnp.zeros((1, NOBS), F32))
        got = mm_nt(lines, pick[...])
        lon_diff = lon_distance(lon0, join(got, 3))
        weight = join(got, 6) / (MEM - 1.0)
        for i in range(CL):
            near_taper[i] = lat_taper(lat0 + i, join(got, 0), lon_diff, weight)

    def update_all():
        loads[-1].wait()
        a, s, _ = gather(packed[0], pick0[...], factor_out[...])
        apack[...] = a
        spack[...] = s

        def rows_of(step, carry):
            lats = pl.ds(step * TL, TL)
            old = state[lats]
            ens[lats] = old + increment(old, apack[...], spack[...], taper0[lats])
            return carry

        lax.fori_loop(0, CL // TL, rows_of, 0)

    def centre(bi, core):
        half = span_of(core)
        for k in range(HB):
            lanes = pl.ds(pl.multiple_of((core * HB + k) * BLK, BLK), BLK)
            block = observed[bi, core * HB + k]
            mean = jnp.sum(block, axis=0, keepdims=True) / MEM
            block = block - mean
            innovation = value[bi : bi + 1, lanes] - mean
            anom[0:MEM, lanes] = block
            anom[MEM : MEM + 8, lanes] = jnp.broadcast_to(innovation, (8, BLK))
            hi, lo = split(block)
            packed[bi, 0:MEM, lanes] = hi
            packed[bi, MEM : 2 * MEM, lanes] = lo
            packed[bi, 2 * MEM :, lanes] = meta_lines(st, fr, variance, bi, lanes, BLK, innovation)
        weight = 1.0 / variance[bi : bi + 1, half]
        return mm_nt(anom[0:MEM, half] * weight, anom[:, half], HIGHEST)

    def total(bi, mine, swap):
        swap.wait_recv()
        mine = mine + partial(bi, 1 - c)
        for k in range(HB):
            part[bi, k] = mine[:, k * BLK : (k + 1) * BLK]
        for r, (pq, target) in enumerate(plane):
            rows = pl.ds(pl.multiple_of(pq * ROWS, ROWS), ROWS)
            copy(part.at[bi, :, rows, :], got1.at[bi, r], bi, 1, target).start()
        if bi == 0:
            tapers()
        else:
            update_all()
        copy(got1.at[bi], got1.at[bi], bi, 1, other).wait_recv()
        mine = part[bi, :, members, :]
        for r in range(len(plane)):
            mine = mine + got1[bi, r]
        got2[bi, z] = mine
        for target in line:
            copy(got2.at[bi, z], got2.at[bi, z], bi, 2, target).start()
        if bi == 0:
            select(0, pick0, taper0)
        seven = got2.at[bi, pl.ds(0, NZ - 1)]
        copy(seven, seven, bi, 2, other).wait_recv()
        mine = got2[bi, 0]
        for r in range(1, NZ):
            mine = mine + got2[bi, r]
        observed[bi, blocks, members, :] = mine
        own = observed.at[bi, blocks, members, :]
        for _, target in plane:
            copy(own, own, bi, 3, target).start()
        if bi == 0:
            select(1, pick1, taper1)
        copy(got1.at[bi], got1.at[bi], bi, 3, other).wait_recv()
        half = observed.at[bi, blocks]
        copy(half, half, bi, 4, other).start()
        gram = centre(bi, c)
        copy(half, half, bi, 4, other).wait_recv()
        return gram + centre(bi, 1 - c)

    def swap_of(bi):
        return copy(surf.at[bi, c], surf.at[bi, c], bi, 0, other)

    mine = partial(0, c)
    pl.semaphore_wait(barrier, len(partners))
    swap_of(0).start()
    gram = total(0, mine, swap_of(0))

    m = gram[:, 0:MEM] + eye(MEM - 1.0)
    xy, low = inverse_start(m)
    for i in range(EXACT + PACKED):
        xy, low = inverse_step(xy, low, i < EXACT)
    factor = spread_factor(inverse_finish(m, xy[0:MEM, :]), gram[:, MEM : MEM + 1])
    factor_out[...] = factor

    surface = surf[0, c].reshape(CL * CL, MEM)
    a_hi, a_lo = split(surface - jnp.mean(surface, axis=-1, keepdims=True))
    b_hi, b_lo = packed[0, 0:MEM, :], packed[0, MEM : 2 * MEM, :]
    cov = mm(a_hi, b_hi) + (mm(a_lo, b_hi) + mm(a_hi, b_lo))
    cov_hi, cov_lo = split(cov * taper[...])
    s_hi, s_lo = split(anom[MEM : MEM + 1, :] - dot(factor, anom[0:MEM, :]))
    delta = mm_nt(cov_hi, s_hi) + (mm_nt(cov_lo, s_hi) + mm_nt(cov_hi, s_lo))
    surf[1, c] = (surface + delta).reshape(CL, CL, MEM)

    swap_of(1).start()
    gram_out[...] = total(1, partial(1, c), swap_of(1))

    for bi in range(2):
        swap_of(bi).wait_send()
        copy(got1.at[bi], got1.at[bi], bi, 1, other).wait_send()
        seven = got2.at[bi, pl.ds(0, NZ - 1)]
        copy(seven, seven, bi, 2, other).wait_send()
        copy(got1.at[bi], got1.at[bi], bi, 3, other).wait_send()
        copy(observed.at[bi, blocks], observed.at[bi, blocks], bi, 4, other).wait_send()


def in_hbm(*arrays):
    return [pltpu.with_memory_space_constraint(a, pltpu.HBM) for a in arrays]


def observe(ens, st, fr, value, variance):
    batches = st.shape[0]
    outs = (
        (ens.shape, F32),
        ((batches, 2 * MEM + META, NOBS), BF16),
        ((batches, NB, BLK), F32),
        ((BLK, NOBS), BF16),
        ((CL, CL, BLK), F32),
        ((MEM, MEM + 8), F32),
        ((MEM, MEM), F32),
    )
    return pl.pallas_call(
        observe_kernel,
        out_shape=tuple(jax.ShapeDtypeStruct(*o) for o in outs),
        in_specs=[pl.BlockSpec(memory_space=pltpu.HBM)] * 5,
        out_specs=tuple(pl.BlockSpec(memory_space=pltpu.VMEM) for _ in outs),
        scratch_shapes=[
            pltpu.VMEM(ens.shape, F32),
            pltpu.VMEM(st.shape, jnp.int32),
            pltpu.VMEM(fr.shape, F32),
            pltpu.VMEM(value.shape, F32),
            pltpu.VMEM(variance.shape, F32),
            pltpu.VMEM((batches, NC, CL, CL, MEM), F32),
            pltpu.VMEM((batches, HB, MEM, BLK), F32),
            pltpu.VMEM((batches, NX * NY - 1, HB, ROWS, BLK), F32),
            pltpu.VMEM((batches, NZ, HB, ROWS, BLK), F32),
            pltpu.VMEM((batches, NB, MEM, BLK), F32),
            pltpu.VMEM((MEM + 8, NOBS), F32),
            pltpu.VMEM((CL * CL, NOBS), F32),
            pltpu.VMEM((BLK, NOBS), BF16),
            pltpu.VMEM((CL, CL, BLK), F32),
            pltpu.VMEM((2 * MEM, 2 * BLK), BF16),
            pltpu.VMEM((2 * BLK, 2 * MEM), BF16),
            pltpu.SemaphoreType.DMA((6,)),
            pltpu.SemaphoreType.DMA((batches, 5)),
            pltpu.SemaphoreType.DMA((batches, 5)),
        ],
        compiler_params=pltpu.CompilerParams(
            collective_id=0, has_side_effects=True, vmem_limit_bytes=36 << 20
        ),
        name="observe",
    )(*in_hbm(ens, st, fr, value, variance))


def update_kernel(
    prior, ens, packed, chosen, pick1, taper1, gram, factor0, out,
    work, factor1, apack, spack, taper, base, staged, sems,
):
    x, y, z, c = place()
    lat0 = ((x * NZ + z) * CL).astype(F32)
    lon0 = ((y * NC + c) * CL).astype(F32)

    m = gram[:, 0:MEM] + eye(MEM - 1.0)
    xy, low = inverse_start(m)
    work[...] = xy

    def step(exact, low):
        xy, low = inverse_step(work[...], jnp.full((1, 1), low, F32), exact)
        work[...] = xy
        return low[0, 0]

    low = lax.while_loop(lambda v: v < 0.001, functools.partial(step, True), low[0, 0])
    lax.while_loop(lambda v: v < 0.999, functools.partial(step, False), low)
    factor1[...] = spread_factor(inverse_finish(m, work[0:MEM, :]), gram[:, MEM : MEM + 1])

    def chunks_of(bi):
        return (jnp.max(chosen[bi]).astype(jnp.int32) + BLK) // BLK

    chunks = chunks_of(0), chunks_of(1)
    short = jnp.maximum(chunks[0], chunks[1]) <= 1

    def rest(bi, start, factor):
        def one(chunk, carry):
            a, s, lines = gather(packed[bi], one_hot(chosen[bi], chunk), factor[...])
            apack[...] = a
            spack[...] = s
            lon_diff = lon_distance(lon0, join(lines, 3))
            weight = join(lines, 6) / (MEM - 1.0)
            for i in range(CL):
                taper[i] = lat_taper(lat0 + i, join(lines, 0), lon_diff, weight)

            def rows_of(step, carry):
                lats = pl.ds(step * TL, TL)
                staged[lats] += increment(base[lats], apack[...], spack[...], taper[lats])
                return carry

            lax.fori_loop(0, CL // TL, rows_of, 0)
            return carry

        lax.fori_loop(start, chunks[bi], one, 0)

    @pl.when(short)
    def _():
        a, s, _ = gather(packed[1], pick1[...], factor1[...])
        apack[...] = a
        spack[...] = s
        writes = []
        for i in range(CL // TL):
            lats = slice(i * TL, (i + 1) * TL)
            old = ens[lats]
            staged[lats] = old + increment(old, apack[...], spack[...], taper1[lats])
            writes.append(pltpu.make_async_copy(staged.at[lats], out.at[lats], sems.at[i]))
            writes[-1].start()
        for one in writes:
            one.wait()

    @pl.when(jnp.logical_not(short))
    def _():
        pltpu.sync_copy(prior, base)
        staged[...] = ens[...]
        rest(0, 1, factor0)
        base[...] = staged[...]
        rest(1, 0, factor1)
        pltpu.sync_copy(staged, out)


def update(prior, ens, packed, chosen, pick1, taper1, gram, factor0):
    vmem = pl.BlockSpec(memory_space=pltpu.VMEM)
    hbm = pl.BlockSpec(memory_space=pltpu.HBM)
    return pl.pallas_call(
        update_kernel,
        out_shape=jax.ShapeDtypeStruct(prior.shape, F32),
        in_specs=[hbm] + [vmem] * 7,
        out_specs=hbm,
        scratch_shapes=[
            pltpu.VMEM((2 * MEM, MEM), F32),
            pltpu.VMEM((MEM, MEM), F32),
            pltpu.VMEM((2 * MEM, 2 * BLK), BF16),
            pltpu.VMEM((2 * BLK, 2 * MEM), BF16),
            pltpu.VMEM((CL, CL, BLK), F32),
            pltpu.VMEM(prior.shape, F32),
            pltpu.VMEM(prior.shape, F32),
            pltpu.SemaphoreType.DMA((CL // TL,)),
        ],
        compiler_params=pltpu.CompilerParams(vmem_limit_bytes=40 << 20),
        name="update",
    )(*in_hbm(prior), ens, packed, chosen, pick1, taper1, gram, factor0)


def local(prior, stencil_rows, obs_frac, obs_value, obs_var):
    st = jnp.transpose(stencil_rows, (0, 2, 1))
    fr = jnp.transpose(obs_frac, (0, 2, 1))
    return update(prior, *observe(prior, st, fr, obs_value, obs_var))


def solution(mesh):
    placed = (P("lat", "lon", None, None), P(), P(), P(), P())
    return jax.shard_map(
        local, mesh=mesh, in_specs=placed, out_specs=P("lat", "lon", None, None), check_vma=False
    )
```

time: 76.6 us -> 63 us (0.82)
  Pallas kernels: 71.8 us -> 62.9 us
  local copies, waits for them, and re-layouts: 4.47 us -> 0 us
    pallas_call x2, Pallas kernels: 71.8 us -> 62.9 us  [the longest x1 58.2 us: observe(): pl.pallas_call(observe_kernel, out_shape=tuple((jax.ShapeDtypeStruct(*o)...]
    unnamed x18 -> x0, local copies, waits for them, and re-layouts: 4.47 us -> none
where the time goes in v3:
time: 63 us; the launch traced here: 62.9 us
  Pallas kernels  62.9 us (100%)
    pallas_call x1, Pallas kernels, observe(): pl.pallas_call(observe_kernel, out_shape=tuple((jax.ShapeDtypeStruct(*o)...  58.2 us
    pallas_call x1, Pallas kernels, update(): pl.pallas_call(update_kernel, out_shape=jax.ShapeDtypeStruct(prior.shape,...  4.72 us

profile of v3, /device:TPU:1, one launch (start us, length us, event | category | flops | bytes accessed | tf_op | source)
XLA Modules:
  0.0 62.9 jit_solution(2735996896581935422)
XLA Ops:
  0.0 58.2 %observe.1 = (f32[16,16,16,128]{3,2,1,0:T(8,128)S(1)}, bf16[2,272,1024]{2,1,0:T(8,128)(2,1)S(1)}, f32[2,8,128]{2,1,0:T(8,128)S(1)}, bf16[128,1024]{1,0:T(8,128)(...) custom-call(f32[16,16,16,128]{3,2,1,0:T(8,128)} %prior.1, ...), custom_call_target="tpu_custom_call" | custom-call | tf_op jit(solution)/shard_map/observe/pallas_call | solution.py:405
  58.2 4.7 %update.1 = f32[16,16,16,128]{3,2,1,0:T(8,128)} custom-call(f32[16,16,16,128]{3,2,1,0:T(8,128)} %prior.1, f32[16,16,16,128]{3,2,1,0:T(8,128)S(1)} %get-tuple-element.12.ens, bf16[2,272,1024]{2,1,0:T(8,128)(2,1)S(1)} %get-tuple-element.13.packed, f32[2,8,128]{2,1,0:T(8,128)S(1)} %get-tuple-element.14.chosen, bf16[128,1024]{1,0:T(8,128)(2,1)S(1)} %get-tuple-element.15.pick1, ...), custom_call_target="tpu_custom_call" | custom-call | tf_op jit(solution)/shard_map/update/pallas_call | solution.py:513

commit v4 on v3

--- a/solution.py
+++ b/solution.py
@@ -21,7 +21,7 @@
 HB = NB // NC
 ROWS = 8
 TL = 4
-EXACT, PACKED = 4, 7
+EXACT, PACKED = 2, 9
 META = 16
 
 
@@ -52,6 +52,10 @@
     return lat // NZ, lon // NC, lat % NZ, lon % NC
 
 
+def hops(step, size):
+    return min(step, size - step)
+
+
 def device(x, y, z, c):
     return (x * NZ + z, y * NC + c)
 
@@ -70,7 +74,7 @@
 def inverse_start(m):
     bound = jnp.max(jnp.sum(jnp.abs(m), axis=0, keepdims=True), axis=1, keepdims=True)
     scale = 1.0 / bound
-    return jnp.concatenate([eye(1.0) * scale, m * scale], axis=0), (MEM - 1.0) * scale
+    return eye(1.0) * scale, m * scale, (MEM - 1.0) * scale
 
 
 def pack_left(v):
@@ -88,12 +92,15 @@
     return both[:, 0:n] + both[:, n:]
 
 
-def inverse_step(xy, low, exact):
+def inverse_step(x, y, low, exact):
     s = jnp.minimum(2.0 / (1.0 + low), 1.95)
-    z = eye(2.0) * s - xy[MEM:, :] * (s * s)
+    z = eye(2.0) * s - y * (s * s)
     t = s * low
     low = jnp.minimum(t * (2.0 - t), s * (2.0 - s))
-    return (dot(xy, z) if exact else packed_dot(pack_left(xy), pack_right(z))), low
+    if exact:
+        return dot(x, z), dot(y, z), low
+    right = pack_right(z)
+    return packed_dot(pack_left(x), right), packed_dot(pack_left(y), right), low
 
 
 def inverse_finish(m, x):
@@ -175,17 +182,19 @@
     ens_in, st_in, fr_in, value_in, var_in,
     ens, packed, chosen, pick1, taper1, gram_out, factor_out,
     state, st, fr, value, variance, surf, part, got1, got2, observed, anom, taper, pick0, taper0,
-    apack, spack, load, send, recv,
+    apack, spack, wts, gram, load, send, recv,
 ):
     x, y, z, c = place()
     q = x * NY + y
     lat0 = ((x * NZ + z) * CL).astype(F32)
     lon0 = ((y * NC + c) * CL).astype(F32)
     plane = []
-    for r in range(1, NX * NY):
+    far = sorted(range(1, NX * NY), key=lambda r: -hops(r // NY, NX) - hops(r % NY, NY))
+    for r in far:
         px, py = lax.rem(x + r // NY, NX), lax.rem(y + r % NY, NY)
         plane.append((px * NY + py, device(px, py, z, c)))
-    line = [device(x, y, lax.rem(z + r, NZ), c) for r in range(1, NZ)]
+    far = sorted(range(1, NZ), key=lambda r: -hops(r, NZ))
+    line = [device(x, y, lax.rem(z + r, NZ), c) for r in far]
     other = device(x, y, z, 1 - c)
 
     def copy(src, dst, bi, stage, target):
@@ -199,7 +208,9 @@
         )
 
     barrier = pltpu.get_barrier_semaphore()
-    partners = [other] + [d for _, d in plane] + line
+    partners = line + [d for _, d in plane] + [other]
+    for target in partners:
+        pl.semaphore_signal(barrier, inc=1, device_id=target, device_id_type=MESH)
     loads = [
         pltpu.make_async_copy(ens_in.at[:, :, 0, :], surf.at[0, c], load.at[0]),
         pltpu.make_async_copy(st_in, st, load.at[1]),
@@ -210,8 +221,6 @@
     ]
     for one in loads:
         one.start()
-    for target in partners:
-        pl.semaphore_signal(barrier, inc=1, device_id=target, device_id_type=MESH)
     for one in loads[:-1]:
         one.wait()
 
@@ -223,7 +232,7 @@
     members = pl.ds(pl.multiple_of(q * ROWS, ROWS), ROWS)
     blocks = pl.ds(c * HB, HB)
 
-    def partial(bi, core):
+    def weights(bi, core):
         first = st[bi, 0:1, span]
         base_lat = lax.shift_right_logical(first, 11)
         base_lon = lax.shift_right_logical(first, 4) & (NLON - 1)
@@ -233,9 +242,11 @@
         lon = cells + (y * NC + core) * CL
         w_lat = jnp.where(lat == base_lat, 1.0 - fa, jnp.where(lat == base_lat + 1, fa, 0.0))
         w_lon = jnp.where(lon == base_lon, 1.0 - fo, jnp.where(lon == east, fo, 0.0))
-        w = (w_lat[:, None, :] * w_lon[None, :, :]).reshape(CL * CL, HB * BLK)
+        return split((w_lat[:, None, :] * w_lon[None, :, :]).reshape(CL * CL, HB * BLK))
+
+    def partial(bi, core):
+        w_hi, w_lo = weights(bi, core) if bi == 0 else (wts[core, 0], wts[core, 1])
         s_hi, s_lo = split(surf[bi, core].reshape(CL * CL, MEM).T)
-        w_hi, w_lo = split(w)
         return mm(s_hi, w_hi) + (mm(s_lo, w_hi) + mm(s_hi, w_lo))
 
     def tapers():
@@ -296,7 +307,6 @@
         lax.fori_loop(0, CL // TL, rows_of, 0)
 
     def centre(bi, core):
-        half = span_of(core)
         for k in range(HB):
             lanes = pl.ds(pl.multiple_of((core * HB + k) * BLK, BLK), BLK)
             block = observed[bi, core * HB + k]
@@ -309,8 +319,12 @@
             packed[bi, 0:MEM, lanes] = hi
             packed[bi, MEM : 2 * MEM, lanes] = lo
             packed[bi, 2 * MEM :, lanes] = meta_lines(st, fr, variance, bi, lanes, BLK, innovation)
-        weight = 1.0 / variance[bi : bi + 1, half]
-        return mm_nt(anom[0:MEM, half] * weight, anom[:, half], HIGHEST)
+
+    def surface_sums(core):
+        half = span_of(core)
+        b_hi, b_lo = packed[0, 0:MEM, half], packed[0, MEM : 2 * MEM, half]
+        cov = mm(a_hi, b_hi) + (mm(a_lo, b_hi) + mm(a_hi, b_lo))
+        return mm_nt(cov * taper[:, half], anom[:, half], HIGHEST)
 
     def total(bi, mine, swap):
         swap.wait_recv()
@@ -344,39 +358,44 @@
             copy(own, own, bi, 3, target).start()
         if bi == 0:
             select(1, pick1, taper1)
+            for core in range(NC):
+                wts[core, 0], wts[core, 1] = weights(1, core)
         copy(got1.at[bi], got1.at[bi], bi, 3, other).wait_recv()
         half = observed.at[bi, blocks]
         copy(half, half, bi, 4, other).start()
-        gram = centre(bi, c)
+        centre(bi, c)
+        weight = 1.0 / variance[bi : bi + 1, span]
+        gram[bi, c] = mm_nt(anom[0:MEM, span] * weight, anom[:, span], HIGHEST)
+        copy(gram.at[bi, c], gram.at[bi, c], bi, 5, other).start()
+        sums = surface_sums(c) if bi == 0 else None
         copy(half, half, bi, 4, other).wait_recv()
-        return gram + centre(bi, 1 - c)
+        centre(bi, 1 - c)
+        copy(gram.at[bi, c], gram.at[bi, c], bi, 5, other).wait_recv()
+        if bi == 0:
+            sums = sums + surface_sums(1 - c)
+        return gram[bi, 0] + gram[bi, 1], sums
 
     def swap_of(bi):
         return copy(surf.at[bi, c], surf.at[bi, c], bi, 0, other)
 
     mine = partial(0, c)
+    surface = surf[0, c].reshape(CL * CL, MEM)
+    a_hi, a_lo = split(surface - jnp.mean(surface, axis=-1, keepdims=True))
     pl.semaphore_wait(barrier, len(partners))
     swap_of(0).start()
-    gram = total(0, mine, swap_of(0))
-
-    m = gram[:, 0:MEM] + eye(MEM - 1.0)
-    xy, low = inverse_start(m)
+    normal, sums = total(0, mine, swap_of(0))
+
+    m = normal[:, 0:MEM] + eye(MEM - 1.0)
+    x_now, y_now, low = inverse_start(m)
     for i in range(EXACT + PACKED):
-        xy, low = inverse_step(xy, low, i < EXACT)
-    factor = spread_factor(inverse_finish(m, xy[0:MEM, :]), gram[:, MEM : MEM + 1])
+        x_now, y_now, low = inverse_step(x_now, y_now, low, i < EXACT)
+    factor = spread_factor(inverse_finish(m, x_now), normal[:, MEM : MEM + 1])
     factor_out[...] = factor
-
-    surface = surf[0, c].reshape(CL * CL, MEM)
-    a_hi, a_lo = split(surface - jnp.mean(surface, axis=-1, keepdims=True))
-    b_hi, b_lo = packed[0, 0:MEM, :], packed[0, MEM : 2 * MEM, :]
-    cov = mm(a_hi, b_hi) + (mm(a_lo, b_hi) + mm(a_hi, b_lo))
-    cov_hi, cov_lo = split(cov * taper[...])
-    s_hi, s_lo = split(anom[MEM : MEM + 1, :] - dot(factor, anom[0:MEM, :]))
-    delta = mm_nt(cov_hi, s_hi) + (mm_nt(cov_lo, s_hi) + mm_nt(cov_hi, s_lo))
-    surf[1, c] = (surface + delta).reshape(CL, CL, MEM)
+    delta = sums[:, MEM : MEM + 1] - mm_nt(sums[:, 0:MEM], factor, HIGHEST)
+    surf[1, c] = (surf[0, c].reshape(CL * CL, MEM) + delta).reshape(CL, CL, MEM)
 
     swap_of(1).start()
-    gram_out[...] = total(1, partial(1, c), swap_of(1))
+    gram_out[...], _ = total(1, partial(1, c), swap_of(1))
 
     for bi in range(2):
         swap_of(bi).wait_send()
@@ -385,6 +404,7 @@
         copy(seven, seven, bi, 2, other).wait_send()
         copy(got1.at[bi], got1.at[bi], bi, 3, other).wait_send()
         copy(observed.at[bi, blocks], observed.at[bi, blocks], bi, 4, other).wait_send()
+        copy(gram.at[bi, c], gram.at[bi, c], bi, 5, other).wait_send()
 
 
 def in_hbm(*arrays):
@@ -424,9 +444,11 @@
             pltpu.VMEM((CL, CL, BLK), F32),
             pltpu.VMEM((2 * MEM, 2 * BLK), BF16),
             pltpu.VMEM((2 * BLK, 2 * MEM), BF16),
+            pltpu.VMEM((NC, 2, CL * CL, HB * BLK), BF16),
+            pltpu.VMEM((batches, NC, MEM, MEM + 8), F32),
             pltpu.SemaphoreType.DMA((6,)),
-            pltpu.SemaphoreType.DMA((batches, 5)),
-            pltpu.SemaphoreType.DMA((batches, 5)),
+            pltpu.SemaphoreType.DMA((batches, 6)),
+            pltpu.SemaphoreType.DMA((batches, 6)),
         ],
         compiler_params=pltpu.CompilerParams(
             collective_id=0, has_side_effects=True, vmem_limit_bytes=36 << 20
@@ -444,17 +466,15 @@
     lon0 = ((y * NC + c) * CL).astype(F32)
 
     m = gram[:, 0:MEM] + eye(MEM - 1.0)
-    xy, low = inverse_start(m)
-    work[...] = xy
+    work[0], work[1], low = inverse_start(m)
 
     def step(exact, low):
-        xy, low = inverse_step(work[...], jnp.full((1, 1), low, F32), exact)
-        work[...] = xy
+        work[0], work[1], low = inverse_step(work[0], work[1], jnp.full((1, 1), low, F32), exact)
         return low[0, 0]
 
     low = lax.while_loop(lambda v: v < 0.001, functools.partial(step, True), low[0, 0])
     lax.while_loop(lambda v: v < 0.999, functools.partial(step, False), low)
-    factor1[...] = spread_factor(inverse_finish(m, work[0:MEM, :]), gram[:, MEM : MEM + 1])
+    factor1[...] = spread_factor(inverse_finish(m, work[0]), gram[:, MEM : MEM + 1])
 
     def chunks_of(bi):
         return (jnp.max(chosen[bi]).astype(jnp.int32) + BLK) // BLK
@@ -516,7 +536,7 @@
         in_specs=[hbm] + [vmem] * 7,
         out_specs=hbm,
         scratch_shapes=[
-            pltpu.VMEM((2 * MEM, MEM), F32),
+            pltpu.VMEM((2, MEM, MEM), F32),
             pltpu.VMEM((MEM, MEM), F32),
             pltpu.VMEM((2 * MEM, 2 * BLK), BF16),
             pltpu.VMEM((2 * BLK, 2 * MEM), BF16),

time: 63 us -> 57.9 us (0.919)
  Pallas kernels: 62.9 us -> 57.8 us
    pallas_call x1, Pallas kernels: 58.2 us -> 53.1 us  [observe(): pl.pallas_call(observe_kernel, out_shape=tuple((jax.ShapeDtypeStruct(*o)...]
where the time goes in v4:
time: 57.9 us; the launch traced here: 57.8 us
  Pallas kernels  57.8 us (100%)
    pallas_call x1, Pallas kernels, observe(): pl.pallas_call(observe_kernel, out_shape=tuple((jax.ShapeDtypeStruct(*o)...  53.1 us
    pallas_call x1, Pallas kernels, update(): pl.pallas_call(update_kernel, out_shape=jax.ShapeDtypeStruct(prior.shape,...  4.72 us

profile of v4, /device:TPU:1, one launch (start us, length us, event | category | flops | bytes accessed | tf_op | source)
XLA Modules:
  0.0 57.8 jit_solution(7960443572540440120)
XLA Ops:
  0.0 53.1 %observe.1 = (f32[16,16,16,128]{3,2,1,0:T(8,128)S(1)}, bf16[2,272,1024]{2,1,0:T(8,128)(2,1)S(1)}, f32[2,8,128]{2,1,0:T(8,128)S(1)}, bf16[128,1024]{1,0:T(8,128)(...) custom-call(f32[16,16,16,128]{3,2,1,0:T(8,128)} %prior.1, ...), custom_call_target="tpu_custom_call" | custom-call | tf_op jit(solution)/shard_map/observe/pallas_call | solution.py:425
  53.1 4.7 %update.1 = f32[16,16,16,128]{3,2,1,0:T(8,128)} custom-call(f32[16,16,16,128]{3,2,1,0:T(8,128)} %prior.1, f32[16,16,16,128]{3,2,1,0:T(8,128)S(1)} %get-tuple-element.12.ens, bf16[2,272,1024]{2,1,0:T(8,128)(2,1)S(1)} %get-tuple-element.13.packed, f32[2,8,128]{2,1,0:T(8,128)S(1)} %get-tuple-element.14.chosen, bf16[128,1024]{1,0:T(8,128)(2,1)S(1)} %get-tuple-element.15.pick1, ...), custom_call_target="tpu_custom_call" | custom-call | tf_op jit(solution)/shard_map/update/pallas_call | solution.py:533

commit v5 on v4

--- a/solution.py
+++ b/solution.py
@@ -19,6 +19,8 @@
 BLK = 128
 NB = NOBS // BLK
 HB = NB // NC
+NCH = 2
+BC = HB // NCH
 ROWS = 8
 TL = 4
 EXACT, PACKED = 2, 9
@@ -217,22 +219,28 @@
         pltpu.make_async_copy(fr_in, fr, load.at[2]),
         pltpu.make_async_copy(value_in, value, load.at[3]),
         pltpu.make_async_copy(var_in, variance, load.at[4]),
-        pltpu.make_async_copy(ens_in, state, load.at[5]),
     ]
+    load_state = pltpu.make_async_copy(ens_in, state, load.at[5])
     for one in loads:
         one.start()
-    for one in loads[:-1]:
+    for one in loads:
         one.wait()
+    load_state.start()
 
     def span_of(core):
         return pl.ds(pl.multiple_of(core * (HB * BLK), BLK), HB * BLK)
 
-    span = span_of(c)
-    cells = lax.broadcasted_iota(jnp.int32, (CL, HB * BLK), 0)
+    cells = lax.broadcasted_iota(jnp.int32, (CL, BC * BLK), 0)
     members = pl.ds(pl.multiple_of(q * ROWS, ROWS), ROWS)
-    blocks = pl.ds(c * HB, HB)
-
-    def weights(bi, core):
+
+    def blocks_of(core, ch):
+        return pl.ds(core * HB + ch * BC, BC)
+
+    def lanes_of(core, ch):
+        return pl.ds(pl.multiple_of((core * HB + ch * BC) * BLK, BLK), BC * BLK)
+
+    def weights(bi, core, ch):
+        span = lanes_of(c, ch)
         first = st[bi, 0:1, span]
         base_lat = lax.shift_right_logical(first, 11)
         base_lon = lax.shift_right_logical(first, 4) & (NLON - 1)
@@ -242,12 +250,19 @@
         lon = cells + (y * NC + core) * CL
         w_lat = jnp.where(lat == base_lat, 1.0 - fa, jnp.where(lat == base_lat + 1, fa, 0.0))
         w_lon = jnp.where(lon == base_lon, 1.0 - fo, jnp.where(lon == east, fo, 0.0))
-        return split((w_lat[:, None, :] * w_lon[None, :, :]).reshape(CL * CL, HB * BLK))
-
-    def partial(bi, core):
-        w_hi, w_lo = weights(bi, core) if bi == 0 else (wts[core, 0], wts[core, 1])
-        s_hi, s_lo = split(surf[bi, core].reshape(CL * CL, MEM).T)
+        return split((w_lat[:, None, :] * w_lon[None, :, :]).reshape(CL * CL, BC * BLK))
+
+    def members_by_cells(bi, core):
+        return split(surf[bi, core].reshape(CL * CL, MEM).T)
+
+    def partial(bi, core, ch, parts):
+        s_hi, s_lo = parts
+        w_hi, w_lo = weights(bi, core, ch) if bi == 0 else (wts[core, ch, 0], wts[core, ch, 1])
         return mm(s_hi, w_hi) + (mm(s_lo, w_hi) + mm(s_hi, w_lo))
+
+    def own_partial(bi):
+        parts = members_by_cells(bi, c)
+        return [partial(bi, c, ch, parts) for ch in range(NCH)]
 
     def tapers():
         for k in range(NB):
@@ -293,7 +308,7 @@
             near_taper[i] = lat_taper(lat0 + i, join(got, 0), lon_diff, weight)
 
     def update_all():
-        loads[-1].wait()
+        load_state.wait()
         a, s, _ = gather(packed[0], pick0[...], factor_out[...])
         apack[...] = a
         spack[...] = s
@@ -306,8 +321,8 @@
 
         lax.fori_loop(0, CL // TL, rows_of, 0)
 
-    def centre(bi, core):
-        for k in range(HB):
+    def centre(bi, core, ch):
+        for k in range(ch * BC, (ch + 1) * BC):
             lanes = pl.ds(pl.multiple_of((core * HB + k) * BLK, BLK), BLK)
             block = observed[bi, core * HB + k]
             mean = jnp.sum(block, axis=0, keepdims=True) / MEM
@@ -328,49 +343,65 @@
 
     def total(bi, mine, swap):
         swap.wait_recv()
-        mine = mine + partial(bi, 1 - c)
-        for k in range(HB):
-            part[bi, k] = mine[:, k * BLK : (k + 1) * BLK]
-        for r, (pq, target) in enumerate(plane):
-            rows = pl.ds(pl.multiple_of(pq * ROWS, ROWS), ROWS)
-            copy(part.at[bi, :, rows, :], got1.at[bi, r], bi, 1, target).start()
+        parts = members_by_cells(bi, 1 - c)
+        for ch in range(NCH):
+            sums = mine[ch] + partial(bi, 1 - c, ch, parts)
+            for k in range(BC):
+                part[bi, ch * BC + k] = sums[:, k * BLK : (k + 1) * BLK]
+            for r, (pq, target) in enumerate(plane):
+                rows = pl.ds(pl.multiple_of(pq * ROWS, ROWS), ROWS)
+                src = part.at[bi, pl.ds(ch * BC, BC), rows, :]
+                copy(src, got1.at[bi, ch, r], bi, 2 + ch, target).start()
         if bi == 0:
             tapers()
         else:
             update_all()
-        copy(got1.at[bi], got1.at[bi], bi, 1, other).wait_recv()
-        mine = part[bi, :, members, :]
-        for r in range(len(plane)):
-            mine = mine + got1[bi, r]
-        got2[bi, z] = mine
-        for target in line:
-            copy(got2.at[bi, z], got2.at[bi, z], bi, 2, target).start()
+        for ch in range(NCH):
+            got = got1.at[bi, ch]
+            copy(got, got, bi, 2 + ch, other).wait_recv()
+            sums = part[bi, ch * BC : (ch + 1) * BC, members, :]
+            for r in range(len(plane)):
+                sums = sums + got1[bi, ch, r]
+            got2[bi, ch, z] = sums
+            for target in line:
+                src = got2.at[bi, ch, z]
+                copy(src, src, bi, 2 + NCH + ch, target).start()
         if bi == 0:
             select(0, pick0, taper0)
-        seven = got2.at[bi, pl.ds(0, NZ - 1)]
-        copy(seven, seven, bi, 2, other).wait_recv()
-        mine = got2[bi, 0]
-        for r in range(1, NZ):
-            mine = mine + got2[bi, r]
-        observed[bi, blocks, members, :] = mine
-        own = observed.at[bi, blocks, members, :]
-        for _, target in plane:
-            copy(own, own, bi, 3, target).start()
+        for ch in range(NCH):
+            seven = got2.at[bi, ch, pl.ds(0, NZ - 1)]
+            copy(seven, seven, bi, 2 + NCH + ch, other).wait_recv()
+            sums = got2[bi, ch, 0]
+            for r in range(1, NZ):
+                sums = sums + got2[bi, ch, r]
+            observed[bi, blocks_of(c, ch), members, :] = sums
+            own = observed.at[bi, blocks_of(c, ch), members, :]
+            for _, target in plane:
+                copy(own, own, bi, 2 + 2 * NCH + ch, target).start()
         if bi == 0:
             select(1, pick1, taper1)
             for core in range(NC):
-                wts[core, 0], wts[core, 1] = weights(1, core)
-        copy(got1.at[bi], got1.at[bi], bi, 3, other).wait_recv()
-        half = observed.at[bi, blocks]
-        copy(half, half, bi, 4, other).start()
-        centre(bi, c)
-        weight = 1.0 / variance[bi : bi + 1, span]
-        gram[bi, c] = mm_nt(anom[0:MEM, span] * weight, anom[:, span], HIGHEST)
-        copy(gram.at[bi, c], gram.at[bi, c], bi, 5, other).start()
+                for ch in range(NCH):
+                    wts[core, ch, 0], wts[core, ch, 1] = weights(1, core, ch)
+        normal = None
+        for ch in range(NCH):
+            got = got1.at[bi, ch]
+            copy(got, got, bi, 2 + 2 * NCH + ch, other).wait_recv()
+            rows = observed.at[bi, blocks_of(c, ch)]
+            copy(rows, rows, bi, 2 + 3 * NCH + ch, other).start()
+            centre(bi, c, ch)
+            span = lanes_of(c, ch)
+            weight = 1.0 / variance[bi : bi + 1, span]
+            piece = mm_nt(anom[0:MEM, span] * weight, anom[:, span], HIGHEST)
+            normal = piece if normal is None else normal + piece
+        gram[bi, c] = normal
+        copy(gram.at[bi, c], gram.at[bi, c], bi, 1, other).start()
         sums = surface_sums(c) if bi == 0 else None
-        copy(half, half, bi, 4, other).wait_recv()
-        centre(bi, 1 - c)
-        copy(gram.at[bi, c], gram.at[bi, c], bi, 5, other).wait_recv()
+        for ch in range(NCH):
+            rows = observed.at[bi, blocks_of(c, ch)]
+            copy(rows, rows, bi, 2 + 3 * NCH + ch, other).wait_recv()
+            centre(bi, 1 - c, ch)
+        copy(gram.at[bi, c], gram.at[bi, c], bi, 1, other).wait_recv()
         if bi == 0:
             sums = sums + surface_sums(1 - c)
         return gram[bi, 0] + gram[bi, 1], sums
@@ -378,7 +409,7 @@
     def swap_of(bi):
         return copy(surf.at[bi, c], surf.at[bi, c], bi, 0, other)
 
-    mine = partial(0, c)
+    mine = own_partial(0)
     surface = surf[0, c].reshape(CL * CL, MEM)
     a_hi, a_lo = split(surface - jnp.mean(surface, axis=-1, keepdims=True))
     pl.semaphore_wait(barrier, len(partners))
@@ -395,16 +426,19 @@
     surf[1, c] = (surf[0, c].reshape(CL * CL, MEM) + delta).reshape(CL, CL, MEM)
 
     swap_of(1).start()
-    gram_out[...], _ = total(1, partial(1, c), swap_of(1))
+    gram_out[...], _ = total(1, own_partial(1), swap_of(1))
 
     for bi in range(2):
         swap_of(bi).wait_send()
-        copy(got1.at[bi], got1.at[bi], bi, 1, other).wait_send()
-        seven = got2.at[bi, pl.ds(0, NZ - 1)]
-        copy(seven, seven, bi, 2, other).wait_send()
-        copy(got1.at[bi], got1.at[bi], bi, 3, other).wait_send()
-        copy(observed.at[bi, blocks], observed.at[bi, blocks], bi, 4, other).wait_send()
-        copy(gram.at[bi, c], gram.at[bi, c], bi, 5, other).wait_send()
+        copy(gram.at[bi, c], gram.at[bi, c], bi, 1, other).wait_send()
+        for ch in range(NCH):
+            got = got1.at[bi, ch]
+            copy(got, got, bi, 2 + ch, other).wait_send()
+            seven = got2.at[bi, ch, pl.ds(0, NZ - 1)]
+            copy(seven, seven, bi, 2 + NCH + ch, other).wait_send()
+            copy(got, got, bi, 2 + 2 * NCH + ch, other).wait_send()
+            rows = observed.at[bi, blocks_of(c, ch)]
+            copy(rows, rows, bi, 2 + 3 * NCH + ch, other).wait_send()
 
 
 def in_hbm(*arrays):
@@ -435,8 +469,8 @@
             pltpu.VMEM(variance.shape, F32),
             pltpu.VMEM((batches, NC, CL, CL, MEM), F32),
             pltpu.VMEM((batches, HB, MEM, BLK), F32),
-            pltpu.VMEM((batches, NX * NY - 1, HB, ROWS, BLK), F32),
-            pltpu.VMEM((batches, NZ, HB, ROWS, BLK), F32),
+            pltpu.VMEM((batches, NCH, NX * NY - 1, BC, ROWS, BLK), F32),
+            pltpu.VMEM((batches, NCH, NZ, BC, ROWS, BLK), F32),
             pltpu.VMEM((batches, NB, MEM, BLK), F32),
             pltpu.VMEM((MEM + 8, NOBS), F32),
             pltpu.VMEM((CL * CL, NOBS), F32),
@@ -444,11 +478,11 @@
             pltpu.VMEM((CL, CL, BLK), F32),
             pltpu.VMEM((2 * MEM, 2 * BLK), BF16),
             pltpu.VMEM((2 * BLK, 2 * MEM), BF16),
-            pltpu.VMEM((NC, 2, CL * CL, HB * BLK), BF16),
+            pltpu.VMEM((NC, NCH, 2, CL * CL, BC * BLK), BF16),
             pltpu.VMEM((batches, NC, MEM, MEM + 8), F32),
             pltpu.SemaphoreType.DMA((6,)),
-            pltpu.SemaphoreType.DMA((batches, 6)),
-            pltpu.SemaphoreType.DMA((batches, 6)),
+            pltpu.SemaphoreType.DMA((batches, 2 + 4 * NCH)),
+            pltpu.SemaphoreType.DMA((batches, 2 + 4 * NCH)),
         ],
         compiler_params=pltpu.CompilerParams(
             collective_id=0, has_side_effects=True, vmem_limit_bytes=36 << 20

time: 57.9 us -> 56.4 us (0.974)
  Pallas kernels: 57.8 us -> 56.3 us
    pallas_call x1, Pallas kernels: 53.1 us -> 51.6 us  [observe(): pl.pallas_call(observe_kernel, out_shape=tuple((jax.ShapeDtypeStruct(*o)...]
where the time goes in v5:
time: 56.4 us; the launch traced here: 56.3 us
  Pallas kernels  56.3 us (100%)
    pallas_call x1, Pallas kernels, observe(): pl.pallas_call(observe_kernel, out_shape=tuple((jax.ShapeDtypeStruct(*o)...  51.6 us
    pallas_call x1, Pallas kernels, update(): pl.pallas_call(update_kernel, out_shape=jax.ShapeDtypeStruct(prior.shape,...  4.72 us

profile of v5, /device:TPU:1, one launch (start us, length us, event | category | flops | bytes accessed | tf_op | source)
XLA Modules:
  0.0 56.3 jit_solution(2561420456637578233)
XLA Ops:
  0.0 51.6 %observe.1 = (f32[16,16,16,128]{3,2,1,0:T(8,128)S(1)}, bf16[2,272,1024]{2,1,0:T(8,128)(2,1)S(1)}, f32[2,8,128]{2,1,0:T(8,128)S(1)}, bf16[128,1024]{1,0:T(8,128)(...) custom-call(f32[16,16,16,128]{3,2,1,0:T(8,128)} %prior.1, ...), custom_call_target="tpu_custom_call" | custom-call | tf_op jit(solution)/shard_map/observe/pallas_call | solution.py:459
  51.6 4.7 %update.1 = f32[16,16,16,128]{3,2,1,0:T(8,128)} custom-call(f32[16,16,16,128]{3,2,1,0:T(8,128)} %prior.1, f32[16,16,16,128]{3,2,1,0:T(8,128)S(1)} %get-tuple-element.12.ens, bf16[2,272,1024]{2,1,0:T(8,128)(2,1)S(1)} %get-tuple-element.13.packed, f32[2,8,128]{2,1,0:T(8,128)S(1)} %get-tuple-element.14.chosen, bf16[128,1024]{1,0:T(8,128)(2,1)S(1)} %get-tuple-element.15.pick1, ...), custom_call_target="tpu_custom_call" | custom-call | tf_op jit(solution)/shard_map/update/pallas_call | solution.py:567

commit v6 on v5

--- a/solution.py
+++ b/solution.py
@@ -164,26 +164,34 @@
     )
 
 
-def gather(packed, pick, factor):
+def near_rows(packed, pick):
     got = mm_nt(packed, pick)
-    near_anom = got[0:MEM] + got[MEM : 2 * MEM]
-    lines = got[2 * MEM :]
-    near_spread = (join(lines, 9) - dot(factor, near_anom)).T
-    return pack_right(near_anom), pack_right(near_spread), lines
+    return got[0:MEM] + got[MEM : 2 * MEM], got[2 * MEM :]
+
+
+def near_spread(near_anom, lines, factor):
+    return pack_right((join(lines, 9) - dot(factor, near_anom)).T)
+
+
+def anomaly_parts(state):
+    anomaly = state - jnp.mean(state, axis=-1, keepdims=True)
+    return pack_left(anomaly.reshape(state.shape[0] * CL * DEPTH, MEM))
+
+
+def tapered(parts, apack, taper):
+    cov = packed_dot(parts, apack).reshape(TL, CL, DEPTH, BLK) * taper[:, :, None, :]
+    return pack_left(cov.reshape(TL * CL * DEPTH, BLK))
 
 
 def increment(state, apack, spack, taper):
-    rows = state.shape[0] * CL * DEPTH
-    anomaly = state - jnp.mean(state, axis=-1, keepdims=True)
-    cov = packed_dot(pack_left(anomaly.reshape(rows, MEM)), apack)
-    cov = cov.reshape(state.shape[0], CL, DEPTH, BLK) * taper[:, :, None, :]
-    return packed_dot(pack_left(cov.reshape(rows, BLK)), spack).reshape(state.shape)
+    cov = tapered(anomaly_parts(state), apack, taper)
+    return packed_dot(cov, spack).reshape(state.shape)
 
 
 def observe_kernel(
     ens_in, st_in, fr_in, value_in, var_in,
-    ens, packed, chosen, pick1, taper1, gram_out, factor_out,
-    state, st, fr, value, variance, surf, part, got1, got2, observed, anom, taper, pick0, taper0,
+    ens, packed, chosen, taper1, parts1, near1, apack1, gram_out, factor_out,
+    state, pick1, st, fr, value, variance, surf, part, got1, got2, observed, anom, taper, pick0, taper0,
     apack, spack, wts, gram, load, send, recv,
 ):
     x, y, z, c = place()
@@ -214,18 +222,17 @@
     for target in partners:
         pl.semaphore_signal(barrier, inc=1, device_id=target, device_id_type=MESH)
     loads = [
-        pltpu.make_async_copy(ens_in.at[:, :, 0, :], surf.at[0, c], load.at[0]),
-        pltpu.make_async_copy(st_in, st, load.at[1]),
-        pltpu.make_async_copy(fr_in, fr, load.at[2]),
+        pltpu.make_async_copy(st_in, st, load.at[0]),
+        pltpu.make_async_copy(fr_in, fr, load.at[1]),
+        pltpu.make_async_copy(ens_in.at[:, :, 0, :], surf.at[0, c], load.at[2]),
         pltpu.make_async_copy(value_in, value, load.at[3]),
         pltpu.make_async_copy(var_in, variance, load.at[4]),
     ]
     load_state = pltpu.make_async_copy(ens_in, state, load.at[5])
     for one in loads:
         one.start()
-    for one in loads:
+    for one in loads[:2]:
         one.wait()
-    load_state.start()
 
     def span_of(core):
         return pl.ds(pl.multiple_of(core * (HB * BLK), BLK), HB * BLK)
@@ -309,14 +316,16 @@
 
     def update_all():
         load_state.wait()
-        a, s, _ = gather(packed[0], pick0[...], factor_out[...])
-        apack[...] = a
-        spack[...] = s
+        near_anom, lines = near_rows(packed[0], pick0[...])
+        apack[...] = pack_right(near_anom)
+        spack[...] = near_spread(near_anom, lines, factor_out[...])
 
         def rows_of(step, carry):
             lats = pl.ds(step * TL, TL)
             old = state[lats]
-            ens[lats] = old + increment(old, apack[...], spack[...], taper0[lats])
+            new = old + increment(old, apack[...], spack[...], taper0[lats])
+            ens[lats] = new
+            parts1[step] = anomaly_parts(new)
             return carry
 
         lax.fori_loop(0, CL // TL, rows_of, 0)
@@ -340,6 +349,10 @@
         b_hi, b_lo = packed[0, 0:MEM, half], packed[0, MEM : 2 * MEM, half]
         cov = mm(a_hi, b_hi) + (mm(a_lo, b_hi) + mm(a_hi, b_lo))
         return mm_nt(cov * taper[:, half], anom[:, half], HIGHEST)
+
+    def near_half(core):
+        half = span_of(core)
+        return mm_nt(packed[1, :, half], pick1[:, half])
 
     def total(bi, mine, swap):
         swap.wait_recv()
@@ -396,11 +409,17 @@
             normal = piece if normal is None else normal + piece
         gram[bi, c] = normal
         copy(gram.at[bi, c], gram.at[bi, c], bi, 1, other).start()
-        sums = surface_sums(c) if bi == 0 else None
+        sums = surface_sums(c) if bi == 0 else near_half(c)
         for ch in range(NCH):
             rows = observed.at[bi, blocks_of(c, ch)]
             copy(rows, rows, bi, 2 + 3 * NCH + ch, other).wait_recv()
             centre(bi, 1 - c, ch)
+        if bi == 1:
+            sums = sums + near_half(1 - c)
+            near_anom = sums[0:MEM] + sums[MEM : 2 * MEM]
+            near1[0:MEM, :] = near_anom
+            near1[MEM:, :] = sums[2 * MEM :]
+            apack1[...] = pack_right(near_anom)
         copy(gram.at[bi, c], gram.at[bi, c], bi, 1, other).wait_recv()
         if bi == 0:
             sums = sums + surface_sums(1 - c)
@@ -409,6 +428,9 @@
     def swap_of(bi):
         return copy(surf.at[bi, c], surf.at[bi, c], bi, 0, other)
 
+    for one in loads[2:]:
+        one.wait()
+    load_state.start()
     mine = own_partial(0)
     surface = surf[0, c].reshape(CL * CL, MEM)
     a_hi, a_lo = split(surface - jnp.mean(surface, axis=-1, keepdims=True))
@@ -451,8 +473,10 @@
         (ens.shape, F32),
         ((batches, 2 * MEM + META, NOBS), BF16),
         ((batches, NB, BLK), F32),
-        ((BLK, NOBS), BF16),
         ((CL, CL, BLK), F32),
+        ((CL // TL, TL * CL * DEPTH, 2 * MEM), BF16),
+        ((MEM + META, BLK), F32),
+        ((2 * MEM, 2 * BLK), BF16),
         ((MEM, MEM + 8), F32),
         ((MEM, MEM), F32),
     )
@@ -463,6 +487,7 @@
         out_specs=tuple(pl.BlockSpec(memory_space=pltpu.VMEM) for _ in outs),
         scratch_shapes=[
             pltpu.VMEM(ens.shape, F32),
+            pltpu.VMEM((BLK, NOBS), BF16),
             pltpu.VMEM(st.shape, jnp.int32),
             pltpu.VMEM(fr.shape, F32),
             pltpu.VMEM(value.shape, F32),
@@ -492,22 +517,30 @@
 
 
 def update_kernel(
-    prior, ens, packed, chosen, pick1, taper1, gram, factor0, out,
-    work, factor1, apack, spack, taper, base, staged, sems,
+    prior, ens, packed, chosen, taper1, parts1, near1, apack1, gram, factor0, out,
+    work, factor1, apack, spack, cov, taper, base, staged, sems,
 ):
     x, y, z, c = place()
     lat0 = ((x * NZ + z) * CL).astype(F32)
     lon0 = ((y * NC + c) * CL).astype(F32)
+    tiles = CL // TL
 
     m = gram[:, 0:MEM] + eye(MEM - 1.0)
-    work[0], work[1], low = inverse_start(m)
-
-    def step(exact, low):
-        work[0], work[1], low = inverse_step(work[0], work[1], jnp.full((1, 1), low, F32), exact)
+    x_now, y_now, low = inverse_start(m)
+
+    def covariances(tile):
+        cov[tile] = tapered(parts1[tile], apack1[...], taper1[tile * TL : (tile + 1) * TL])
+
+    def step(low):
+        work[0], work[1], low = inverse_step(work[0], work[1], jnp.full((1, 1), low, F32), False)
         return low[0, 0]
 
-    low = lax.while_loop(lambda v: v < 0.001, functools.partial(step, True), low[0, 0])
-    lax.while_loop(lambda v: v < 0.999, functools.partial(step, False), low)
+    for i in range(EXACT + 3):
+        x_now, y_now, low = inverse_step(x_now, y_now, low, i < EXACT)
+        if i < tiles:
+            covariances(i)
+    work[0], work[1] = x_now, y_now
+    lax.while_loop(lambda low: low < 0.999, step, low[0, 0])
     factor1[...] = spread_factor(inverse_finish(m, work[0]), gram[:, MEM : MEM + 1])
 
     def chunks_of(bi):
@@ -518,9 +551,9 @@
 
     def rest(bi, start, factor):
         def one(chunk, carry):
-            a, s, lines = gather(packed[bi], one_hot(chosen[bi], chunk), factor[...])
-            apack[...] = a
-            spack[...] = s
+            near_anom, lines = near_rows(packed[bi], one_hot(chosen[bi], chunk))
+            apack[...] = pack_right(near_anom)
+            spack[...] = near_spread(near_anom, lines, factor[...])
             lon_diff = lon_distance(lon0, join(lines, 3))
             weight = join(lines, 6) / (MEM - 1.0)
             for i in range(CL):
@@ -538,14 +571,12 @@
 
     @pl.when(short)
     def _():
-        a, s, _ = gather(packed[1], pick1[...], factor1[...])
-        apack[...] = a
-        spack[...] = s
+        spack[...] = near_spread(near1[0:MEM, :], near1[MEM:, :], factor1[...])
         writes = []
-        for i in range(CL // TL):
+        for i in range(tiles):
             lats = slice(i * TL, (i + 1) * TL)
             old = ens[lats]
-            staged[lats] = old + increment(old, apack[...], spack[...], taper1[lats])
+            staged[lats] = old + packed_dot(cov[i], spack[...]).reshape(old.shape)
             writes.append(pltpu.make_async_copy(staged.at[lats], out.at[lats], sems.at[i]))
             writes[-1].start()
         for one in writes:
@@ -561,19 +592,20 @@
         pltpu.sync_copy(staged, out)
 
 
-def update(prior, ens, packed, chosen, pick1, taper1, gram, factor0):
+def update(prior, *summed):
     vmem = pl.BlockSpec(memory_space=pltpu.VMEM)
     hbm = pl.BlockSpec(memory_space=pltpu.HBM)
     return pl.pallas_call(
         update_kernel,
         out_shape=jax.ShapeDtypeStruct(prior.shape, F32),
-        in_specs=[hbm] + [vmem] * 7,
+        in_specs=[hbm] + [vmem] * len(summed),
         out_specs=hbm,
         scratch_shapes=[
             pltpu.VMEM((2, MEM, MEM), F32),
             pltpu.VMEM((MEM, MEM), F32),
             pltpu.VMEM((2 * MEM, 2 * BLK), BF16),
             pltpu.VMEM((2 * BLK, 2 * MEM), BF16),
+            pltpu.VMEM((CL // TL, TL * CL * DEPTH, 2 * BLK), BF16),
             pltpu.VMEM((CL, CL, BLK), F32),
             pltpu.VMEM(prior.shape, F32),
             pltpu.VMEM(prior.shape, F32),
@@ -581,7 +613,7 @@
         ],
         compiler_params=pltpu.CompilerParams(vmem_limit_bytes=40 << 20),
         name="update",
-    )(*in_hbm(prior), ens, packed, chosen, pick1, taper1, gram, factor0)
+    )(*in_hbm(prior), *summed)
 
 
 def local(prior, stencil_rows, obs_frac, obs_value, obs_var):

time: 56.4 us -> 56.1 us (level)
  no operation moved by 1% of the time
where the time goes in v6:
time: 56.1 us; the launch traced here: 56 us
  Pallas kernels  56 us (100%)
    pallas_call x1, Pallas kernels, observe(): pl.pallas_call(observe_kernel, out_shape=tuple((jax.ShapeDtypeStruct(*o)...  51.7 us
    pallas_call x1, Pallas kernels, update(): pl.pallas_call(update_kernel, out_shape=jax.ShapeDtypeStruct(prior.shape,...  4.28 us

profile of v6, /device:TPU:1, one launch (start us, length us, event | category | flops | bytes accessed | tf_op | source)
XLA Modules:
  0.0 56.0 jit_solution(12127007428355858887)
XLA Ops:
  0.0 51.7 %observe.1 = (f32[16,16,16,128]{3,2,1,0:T(8,128)S(1)}, bf16[2,272,1024]{2,1,0:T(8,128)(2,1)S(1)}, f32[2,8,128]{2,1,0:T(8,128)S(1)}, f32[16,16,128]{2,1,0:T(8,128...) custom-call(f32[16,16,16,128]{3,2,1,0:T(8,128)} %prior.1, ...), custom_call_target="tpu_custom_call" | custom-call | tf_op jit(solution)/shard_map/observe/pallas_call | solution.py:483
  51.7 4.3 %update.1 = f32[16,16,16,128]{3,2,1,0:T(8,128)} custom-call(f32[16,16,16,128]{3,2,1,0:T(8,128)} %prior.1, f32[16,16,16,128]{3,2,1,0:T(8,128)S(1)} %get-tuple-element.14.ens, bf16[2,272,1024]{2,1,0:T(8,128)(2,1)S(1)} %get-tuple-element.15.packed, f32[2,8,128]{2,1,0:T(8,128)S(1)} %get-tuple-element.16.chosen, f32[16,16,128]{2,1,0:T(8,128)S(1)} %get-tuple-element.17.taper1, ...), custom_call_target="tpu_custom_call" | custom-call | tf_op jit(solution)/shard_map/update/pallas_call | solution.py:598

commit v7 on v6

--- a/solution.py
+++ b/solution.py
@@ -347,8 +347,14 @@
     def surface_sums(core):
         half = span_of(core)
         b_hi, b_lo = packed[0, 0:MEM, half], packed[0, MEM : 2 * MEM, half]
-        cov = mm(a_hi, b_hi) + (mm(a_lo, b_hi) + mm(a_hi, b_lo))
-        return mm_nt(cov * taper[:, half], anom[:, half], HIGHEST)
+        cov = mm(a_both, jnp.concatenate([b_hi, b_hi], axis=0))
+        cov = cov + mm(a_both, jnp.concatenate([b_lo, b_lo], axis=0))
+        cov = cov * taper[:, half]
+        cov_hi, cov_lo = split(cov)
+        parts = packed[0, 0 : 2 * MEM, half]
+        both = mm_nt(cov_hi, parts) + mm_nt(cov_lo, parts)
+        pull = jnp.sum(cov * anom[MEM : MEM + 1, half], axis=1, keepdims=True)
+        return both[:, 0:MEM] + both[:, MEM:], pull
 
     def near_half(core):
         half = span_of(core)
@@ -422,7 +428,8 @@
             apack1[...] = pack_right(near_anom)
         copy(gram.at[bi, c], gram.at[bi, c], bi, 1, other).wait_recv()
         if bi == 0:
-            sums = sums + surface_sums(1 - c)
+            more = surface_sums(1 - c)
+            sums = sums[0] + more[0], sums[1] + more[1]
         return gram[bi, 0] + gram[bi, 1], sums
 
     def swap_of(bi):
@@ -433,7 +440,7 @@
     load_state.start()
     mine = own_partial(0)
     surface = surf[0, c].reshape(CL * CL, MEM)
-    a_hi, a_lo = split(surface - jnp.mean(surface, axis=-1, keepdims=True))
+    a_both = pack_left(surface - jnp.mean(surface, axis=-1, keepdims=True))
     pl.semaphore_wait(barrier, len(partners))
     swap_of(0).start()
     normal, sums = total(0, mine, swap_of(0))
@@ -444,7 +451,7 @@
         x_now, y_now, low = inverse_step(x_now, y_now, low, i < EXACT)
     factor = spread_factor(inverse_finish(m, x_now), normal[:, MEM : MEM + 1])
     factor_out[...] = factor
-    delta = sums[:, MEM : MEM + 1] - mm_nt(sums[:, 0:MEM], factor, HIGHEST)
+    delta = sums[1] - mm_nt(sums[0], factor, HIGHEST)
     surf[1, c] = (surf[0, c].reshape(CL * CL, MEM) + delta).reshape(CL, CL, MEM)
 
     swap_of(1).start()

time: 56.1 us -> 56 us (level)
  no operation moved by 1% of the time
where the time goes in v7:
time: 56 us; the launch traced here: 55.9 us
  Pallas kernels  55.9 us (100%)
    pallas_call x1, Pallas kernels, observe(): pl.pallas_call(observe_kernel, out_shape=tuple((jax.ShapeDtypeStruct(*o)...  51.6 us
    pallas_call x1, Pallas kernels, update(): pl.pallas_call(update_kernel, out_shape=jax.ShapeDtypeStruct(prior.shape,...  4.28 us

profile of v7, /device:TPU:1, one launch (start us, length us, event | category | flops | bytes accessed | tf_op | source)
XLA Modules:
  0.0 55.9 jit_solution(15686010580634390913)
XLA Ops:
  0.0 51.6 %observe.1 = (f32[16,16,16,128]{3,2,1,0:T(8,128)S(1)}, bf16[2,272,1024]{2,1,0:T(8,128)(2,1)S(1)}, f32[2,8,128]{2,1,0:T(8,128)S(1)}, f32[16,16,128]{2,1,0:T(8,128...) custom-call(f32[16,16,16,128]{3,2,1,0:T(8,128)} %prior.1, ...), custom_call_target="tpu_custom_call" | custom-call | tf_op jit(solution)/shard_map/observe/pallas_call | solution.py:490
  51.6 4.3 %update.1 = f32[16,16,16,128]{3,2,1,0:T(8,128)} custom-call(f32[16,16,16,128]{3,2,1,0:T(8,128)} %prior.1, f32[16,16,16,128]{3,2,1,0:T(8,128)S(1)} %get-tuple-element.14.ens, bf16[2,272,1024]{2,1,0:T(8,128)(2,1)S(1)} %get-tuple-element.15.packed, f32[2,8,128]{2,1,0:T(8,128)S(1)} %get-tuple-element.16.chosen, f32[16,16,128]{2,1,0:T(8,128)S(1)} %get-tuple-element.17.taper1, ...), custom_call_target="tpu_custom_call" | custom-call | tf_op jit(solution)/shard_map/update/pallas_call | solution.py:605

commit v8 on v6

--- a/solution.py
+++ b/solution.py
@@ -573,10 +573,12 @@
     def _():
         spack[...] = near_spread(near1[0:MEM, :], near1[MEM:, :], factor1[...])
         writes = []
-        for i in range(tiles):
-            lats = slice(i * TL, (i + 1) * TL)
+        part = TL // 2
+        for i in range(2 * tiles):
+            lats = slice(i * part, (i + 1) * part)
             old = ens[lats]
-            staged[lats] = old + packed_dot(cov[i], spack[...]).reshape(old.shape)
+            rows = slice(i % 2 * part * CL * DEPTH, (i % 2 + 1) * part * CL * DEPTH)
+            staged[lats] = old + packed_dot(cov[i // 2, rows, :], spack[...]).reshape(old.shape)
             writes.append(pltpu.make_async_copy(staged.at[lats], out.at[lats], sems.at[i]))
             writes[-1].start()
         for one in writes:
@@ -609,7 +611,7 @@
             pltpu.VMEM((CL, CL, BLK), F32),
             pltpu.VMEM(prior.shape, F32),
             pltpu.VMEM(prior.shape, F32),
-            pltpu.SemaphoreType.DMA((CL // TL,)),
+            pltpu.SemaphoreType.DMA((2 * CL // TL,)),
         ],
         compiler_params=pltpu.CompilerParams(vmem_limit_bytes=40 << 20),
         name="update",

time: 56.1 us -> 56 us (level)
  no operation moved by 1% of the time
where the time goes in v8:
time: 56 us; the launch traced here: 55.9 us
  Pallas kernels  55.9 us (100%)
    pallas_call x1, Pallas kernels, observe(): pl.pallas_call(observe_kernel, out_shape=tuple((jax.ShapeDtypeStruct(*o)...  51.7 us
    pallas_call x1, Pallas kernels, update(): pl.pallas_call(update_kernel, out_shape=jax.ShapeDtypeStruct(prior.shape,...  4.15 us

profile of v8, /device:TPU:1, one launch (start us, length us, event | category | flops | bytes accessed | tf_op | source)
XLA Modules:
  0.0 55.9 jit_solution(8572476762204735906)
XLA Ops:
  0.0 51.7 %observe.1 = (f32[16,16,16,128]{3,2,1,0:T(8,128)S(1)}, bf16[2,272,1024]{2,1,0:T(8,128)(2,1)S(1)}, f32[2,8,128]{2,1,0:T(8,128)S(1)}, f32[16,16,128]{2,1,0:T(8,128...) custom-call(f32[16,16,16,128]{3,2,1,0:T(8,128)} %prior.1, ...), custom_call_target="tpu_custom_call" | custom-call | tf_op jit(solution)/shard_map/observe/pallas_call | solution.py:483
  51.7 4.1 %update.1 = f32[16,16,16,128]{3,2,1,0:T(8,128)} custom-call(f32[16,16,16,128]{3,2,1,0:T(8,128)} %prior.1, f32[16,16,16,128]{3,2,1,0:T(8,128)S(1)} %get-tuple-element.14.ens, bf16[2,272,1024]{2,1,0:T(8,128)(2,1)S(1)} %get-tuple-element.15.packed, f32[2,8,128]{2,1,0:T(8,128)S(1)} %get-tuple-element.16.chosen, f32[16,16,128]{2,1,0:T(8,128)S(1)} %get-tuple-element.17.taper1, ...), custom_call_target="tpu_custom_call" | custom-call | tf_op jit(solution)/shard_map/update/pallas_call | solution.py:600
